TPU v7x, 32 devices: a whole 2x2x4 slice. The times are simulated.
32 devices in a mesh: cuts: 16 (over z, y, core), chan: 2 (over x).
Axes of the slice: x: 2, y: 2, z: 4, core: 2. Of those that a mesh axis runs over, the one named last changes fastest.
Arguments:
- data: bfloat16 [128, 384, 1024], P('cuts', None, 'chan'), may hold values from -6 to 6
- order: int32 [128], P('cuts'), may hold values from 0 to 127, as said below
- chan_factor: bfloat16 [1024, 64], P('chan'), may hold values from -0.1875 to 0.1875
- slice_weights: float32 [128, 64], P('cuts'), may hold values from 0.5 to 2
- smooth_aux: float32 [128, 384, 64], P('cuts', 'chan'), may hold values from -6 to 6
- coupled: float32 [128, 384, 64], P('cuts', 'chan'), may hold values from -6 to 6
- smooth_dual: float32 [128, 384, 64], P('cuts', 'chan'), may hold values from -2 to 2
- coupling_dual: float32 [128, 384, 64], P('cuts', 'chan'), may hold values from -2 to 2
- delta: float32 [64, 64], replicated, may hold values from -0.1125 to 1.1125, as said below
Outputs:
- evolving: float32 [128, 384, 64], P('cuts', 'chan')
- coupled_out: float32 [128, 384, 64], P('cuts', 'chan')
- delta_out: float32 [64, 64], replicated
Inputs may be any that keep to these rules, and one draw needn't show every extreme that they name: `order`: within each aligned block of 8 entries (the slices of one index of cuts) the entries are a permutation of that block's own slice indices; entry k names the stored slice of phase bin k. `delta`: A full-rank matrix.
All inputs are finite; a program needn't handle non-finite values.
Results may differ from a plain program's by a relative error of at most 0.0003.
Values sent between devices are 32-bit elements; how exact they have to be, the bound alone decides.
No kernel may reach another device: no remote copies, remote signals or barrier semaphores. Data moves between devices by JAX's collectives and lax.ppermute only.
A program may use at most 64 MiB of HBM per device.

v0:
```python
import functools

import jax
import jax.numpy as jnp
from jax import lax
from jax.experimental import pallas as pl
from jax.experimental.pallas import tpu as pltpu
from jax.sharding import PartitionSpec as P

INNER = 3
SWEEPS = 4
POLAR = 8

smooth_weight = 1.0
eps_trace = 1e-06
f32 = jnp.float32
bf16 = jnp.bfloat16
NN = (((1,), (0,)), ((), ()))
NT = (((1,), (1,)), ((), ()))


def dot(left, right, dims=NN):
    return lax.dot_general(left, right, dims, preferred_element_type=f32)


def split(value):
    high = value.astype(bf16)
    low = (value - high.astype(f32)).astype(bf16)
    return high, low


def left_triple(value):
    high, low = split(value)
    return jnp.concatenate([high, high, low], axis=1)


def right_triple(value):
    high, low = split(value)
    return jnp.concatenate([high, low, high], axis=0)


def block_mask(rank, group):
    wide = rank * group
    rows = lax.div(lax.broadcasted_iota(jnp.int32, (wide, wide), 0), rank)
    cols = lax.div(lax.broadcasted_iota(jnp.int32, (wide, wide), 1), rank)
    return jnp.where(rows == cols, 1.0, 0.0).astype(bf16)


def wide_eye(rank, group):
    rows = lax.broadcasted_iota(jnp.int32, (rank, rank * group), 0)
    cols = lax.broadcasted_iota(jnp.int32, (rank, rank * group), 1)
    return jnp.where(rows == lax.rem(cols, rank), 1.0, 0.0).astype(f32)


def block_diagonal(value, mask, group, dims=NN):
    high, low = [jnp.concatenate([part] * group, axis=0) * mask for part in split(value)]
    return jnp.concatenate([high, low, high], axis=0 if dims == NN else 1)


def times_blocks(values, blocks, dims=NN):
    rank = values[0].shape[0]
    total = dot(jnp.concatenate([left_triple(value) for value in values], axis=0), blocks, dims)
    return [total[at * rank : (at + 1) * rank] for at in range(len(values))]


def diagonal_blocks(value, rank, group):
    at = lax.div(lax.broadcasted_iota(jnp.int32, (rank, rank * group), 1), rank)
    total = value[:rank]
    for block in range(1, group):
        total = jnp.where(at == block, value[block * rank : (block + 1) * rank], total)
    return total


def from_left(left, values):
    wide = values[0].shape[1]
    total = dot(left_triple(left), right_triple(jnp.concatenate(values, axis=1)))
    return [total[:, at * wide : (at + 1) * wide] for at in range(len(values))]


def group_size(count, rank):
    group = max(1, 128 // rank)
    while count % group:
        group -= 1
    return group


def project_kernel(first, pairs, rows, lead, me_ref, data_ref, factor_ref, *refs):
    *outs, held, arrived = refs
    half = data_ref.shape[1] // 2
    copies = []
    for k in range(2 * pairs):
        for at in range(2):
            place = pl.ds(at * half, half)
            copies.append(
                pltpu.make_async_copy(
                    data_ref.at[first + k, place, :], held.at[k, place, :], arrived.at[2 * k + at]
                )
            )
            copies[-1].start()
    factor = factor_ref[...]
    rank = factor.shape[0]
    if lead:
        *outs, again_ref = outs
        again_ref[...] = factor
        gram = dot(factor, factor, NT)
        for out in outs:
            out[pairs * rows :, :] = jnp.concatenate([gram[: rank // 2], gram[rank // 2 :]], axis=1)
    parts = len(outs)
    empty = jnp.zeros_like(factor)
    sides = [
        jnp.concatenate([factor, empty], axis=0),
        jnp.concatenate([empty, factor], axis=0),
    ]
    for pair in range(pairs):
        for copy in copies[4 * pair : 4 * pair + 4]:
            copy.wait()
        for part in reversed(range(parts)):
            start = pl.multiple_of(lax.rem(me_ref[0] + part, parts) * rows, 16)
            place = pl.ds(start, rows)
            outs[part][pair * rows : (pair + 1) * rows, :] = dot(
                held[2 * pair, place, :], sides[0], NT
            ) + dot(held[2 * pair + 1, place, :], sides[1], NT)


def setup_kernel(parts, first, group, order_ref, *refs):
    lead_refs, refs = refs[:parts], refs[parts:]
    (own_ref, aux_ref, coupled_ref, dual_s_ref, dual_c_ref) = refs[:5]
    (inverse_ref, mover_ref, rho_ref, diagonal_ref, columns_ref, base_ref) = refs[5:]
    count, rank = own_ref.shape
    gram = summed(lead_refs, slice(first, None))
    gram = jnp.concatenate([gram[:, :rank], gram[:, rank:]], axis=0)
    eye = wide_eye(rank, 1)
    diagonal = jnp.sum(gram * eye, axis=0, keepdims=True)
    diagonal_ref[...] = jnp.broadcast_to(diagonal, diagonal_ref.shape)
    weights = own_ref[...]
    columns = weights.T
    columns_ref[...] = columns
    rho = jnp.sum(weights * weights * diagonal, axis=1, keepdims=True) / rank
    rho_ref[...] = jnp.broadcast_to(rho, rho_ref.shape)

    centre = rank / 2.0 + 2.0
    edge = centre / (rank / 2.0)
    lead = 4.0 * edge**3 / (4.0 * edge**3 - 3.0 * edge)
    mask = block_mask(rank, group)
    wide = wide_eye(rank, group)
    starts = range(0, count, group)
    systems = []
    for first in starts:
        scaled = []
        for k in range(first, first + group):
            unit = 1.0 / (centre * rho[k : k + 1, :])
            column = columns[:, k : k + 1]
            scaled.append(column * gram * weights[k : k + 1, :] * unit + (2.0 / centre) * eye)
        systems.append(jnp.concatenate(scaled, axis=1))
    inverses, rests = [], []
    for system in systems:
        rest = wide - system
        blocks = block_diagonal(rest, mask, group)
        (square,) = times_blocks([rest], blocks)
        (cube,) = times_blocks([square], blocks)
        inverses.append(wide + lead * (rest + square))
        rests.append(lead * cube - (lead - 1.0) * rest)
    for step in range(5):
        for at in range(len(systems)):
            blocks = block_diagonal(rests[at], mask, group)
            more, *rest = times_blocks([inverses[at], rests[at]][: 2 if step < 4 else 1], blocks)
            inverses[at] = inverses[at] + more
            rests[at] = rest[0] if rest else None
    for at in range(len(systems)):
        (product,) = times_blocks([inverses[at]], block_diagonal(systems[at], mask, group))
        blocks = block_diagonal(wide - product, mask, group)
        (more,) = times_blocks([inverses[at]], blocks)
        inverses[at] = inverses[at] + more
    for k in range(count):
        place = (k % group) * rank
        unit = 1.0 / (centre * rho[k : k + 1, :])
        inverse = inverses[k // group][:, place : place + rank] * unit
        inverse_ref[k] = left_triple(inverse)
        base_ref[k] = dot(
            inverse_ref[k],
            right_triple(
                rho[k : k + 1, :] * (aux_ref[k] - dual_s_ref[k] + coupled_ref[k] - dual_c_ref[k])
            ),
        )
        both = jnp.concatenate([inverse * weights[k : k + 1, :]] * 2, axis=1)
        side = lax.div(lax.broadcasted_iota(jnp.int32, both.shape, 1), rank)
        both = jnp.where(side == lax.rem(order_ref[k], 2), both, 0.0)
        high, low = split(both)
        pair, place = stored_place(order_ref, k, count, rank)
        mover_ref[pair, place, :] = jnp.concatenate([high, high, low], axis=1)


def cross_blocks(lefts, rights, rank):
    group = len(lefts)
    wide = group * rank
    left = jnp.concatenate(split(jnp.concatenate(lefts, axis=0)), axis=0)
    right = left
    if rights is not lefts:
        right = jnp.concatenate(split(jnp.concatenate(rights, axis=0)), axis=0)
    total = dot(left, right, NT)
    total = total[:wide, :wide] + total[:wide, wide:] + total[wide:, :wide]
    return diagonal_blocks(total, rank, group)


def summed(refs, at):
    total = refs[0][at]
    for ref in refs[1:]:
        total = total + ref[at]
    return total


def stored_place(order_ref, k, count, rank):
    stored = lax.rem(order_ref[k], count)
    return lax.div(stored, 2), pl.ds(pl.multiple_of(lax.rem(stored, 2) * rank, rank), rank)


def move(mover, projected):
    high, low = split(projected)
    return dot(mover, jnp.concatenate([high, low, high], axis=1), NT)


def move_kernel(mover_ref, *refs):
    *projected_refs, moved_ref, turned_ref = refs
    rows = moved_ref.shape[2]
    for pair in range(moved_ref.shape[0]):
        projected = summed(projected_refs, slice(pair * rows, (pair + 1) * rows))
        moved_ref[pair] = move(mover_ref[pair], projected)
        turned_ref[pair] = projected.T


def first_kernel(group, order_ref, *refs):
    base_ref, mover_ref, dual_s_ref, dual_c_ref, early_ref = refs[2:7]
    *projected_refs, tall_ref, target_ref, gram_ref, moved = refs[7:]
    count, rank, rows = base_ref.shape
    early = early_ref.shape[0]
    for pair in range(early):
        moved[pair] = early_ref[pair]
    for pair in range(early, count // 2):
        place = slice((pair - early) * rows, (pair - early + 1) * rows)
        moved[pair] = move(mover_ref[pair], summed(projected_refs, place))
    talls = []
    for k in range(count):
        pair, place = stored_place(order_ref, k, count, rank)
        evolving = base_ref[k] + moved[pair, place, :]
        target_ref[k] = evolving + dual_s_ref[k]
        tall = evolving + dual_c_ref[k]
        tall_ref[k] = tall
        talls.append(tall)
        if len(talls) == group:
            gram_ref[k // group] = cross_blocks(talls, talls, rank)
            talls = []


def smooth(odd, now, targets, rho, inside_ref, near_ref, far_ref):
    count = len(targets)
    width = SWEEPS
    share = {j: 2.0 * smooth_weight / (rho[j] + 4.0 * smooth_weight) for j in rho}
    pull = {j: (rho[j] / (rho[j] + 4.0 * smooth_weight)) * targets[j] for j in range(count)}
    now = {j: now[j] for j in range(count)}
    for sweep in range(width):
        later = {}
        for j in range(-sweep - 1, count + sweep + 1):
            beside = [now[i] for i in (j - 1, j + 1) if i in now]
            total = beside[0] if len(beside) == 1 else beside[0] + beside[1]
            total = share[j] * total
            later[j] = total + pull[j] if j in pull else total
        now = later
    for j in range(count):
        inside_ref[j] = now[j]
    rows = inside_ref.shape[2]
    for j in range(width):
        lanes = slice((j % 2) * rows, (j % 2 + 1) * rows)
        near_ref[j // 2, :, lanes] = jnp.where(odd == 1, now[j - width], now[count + j])
        far_ref[j // 2, :, lanes] = jnp.where(odd == 1, now[count + j], now[j - width])


def all_rho(before_ref, rho_ref, after_ref):
    count = rho_ref.shape[0]
    rho = {j: rho_ref[j : j + 1, 0:1] for j in range(count)}
    for j in range(SWEEPS):
        rho[j - SWEEPS] = before_ref[count - SWEEPS + j : count - SWEEPS + j + 1, 0:1]
        rho[count + j] = after_ref[j : j + 1, 0:1]
    return rho


def smooth_kernel(
    odd_ref, order_ref, aux_ref, target_ref, before_ref, rho_ref, after_ref, diagonal_ref,
    columns_ref, early_ref, *refs
):
    *projected_refs, side_ref, past_ref, next_ref, inside_ref, near_ref, far_ref, turned = refs
    count, rank, rows = aux_ref.shape
    for source, place in ((before_ref, past_ref), (after_ref, next_ref)):
        weights = source[...]
        rho = jnp.sum(weights * weights * diagonal_ref[...], axis=1, keepdims=True) / rank
        place[...] = jnp.broadcast_to(rho, place.shape)
    rho = all_rho(past_ref, rho_ref, next_ref)
    slices = range(count)
    smooth(
        odd_ref[0], [aux_ref[k] for k in slices], [target_ref[k] for k in slices], rho,
        inside_ref, near_ref, far_ref,
    )
    early = early_ref.shape[0]
    for pair in range(early):
        turned[pair] = early_ref[pair]
    for pair in range(early, count // 2):
        place = slice((pair - early) * rows, (pair - early + 1) * rows)
        turned[pair] = summed(projected_refs, place).T
    for k in slices:
        pair, place = stored_place(order_ref, k, count, rank)
        side_ref[k] = columns_ref[:, k : k + 1] * turned[pair, place, :]


def polar(grams, delta):
    rank, wide = grams[0].shape
    group = wide // rank
    mask = block_mask(rank, group)
    eye = wide_eye(rank, group)
    delta_wide = jnp.concatenate([delta] * group, axis=1)
    delta_blocks = block_diagonal(delta_wide, mask, group, NT)
    (across,) = from_left(delta.T, [delta_wide])
    traces = []
    for gram in grams:
        line = jnp.broadcast_to(jnp.sum(across * gram, axis=0, keepdims=True), (16, wide))
        high, low = split(line)
        rest = (line - high.astype(f32) - low.astype(f32)).astype(bf16)
        line = dot(high, mask) + dot(low, mask) + dot(rest, mask)
        traces.append(line[0:1] + eps_trace)
    rights = [times_blocks([gram], delta_blocks, NT)[0] for gram in grams]
    normals = from_left(delta, rights)
    currents = [normal / trace for normal, trace in zip(normals, traces)]
    scales = [1.0 / jnp.sqrt(trace) for trace in traces]
    roots = []
    for step in range(POLAR):
        for at in range(len(grams)):
            product = currents[at]
            blocks = block_diagonal(product, mask, group)
            if step == 0:
                roots.append(1.5 * eye - 0.5 * product)
                (square,) = times_blocks([product], blocks)
            elif step < POLAR - 1:
                square, more = times_blocks([product, roots[at]], blocks)
                roots[at] = 1.5 * roots[at] - 0.5 * more
            else:
                (more,) = times_blocks([roots[at]], blocks)
                roots[at] = 1.5 * roots[at] - 0.5 * more
            if step < POLAR - 1:
                half = 1.5 * product - 0.5 * square
                (more,) = times_blocks([half], blocks)
                currents[at] = 1.5 * half - 0.5 * more
    return roots, scales, rights


def mix(roots, scales, rights, delta, mixed_ref, partial_ref):
    rank, wide = roots[0].shape
    group = wide // rank
    mask = block_mask(rank, group)
    delta_blocks = block_diagonal(jnp.concatenate([delta] * group, axis=1), mask, group)
    left, right = [], []
    for at in range(len(roots)):
        high, low = split(roots[at] * scales[at])
        left += [high, high, low]
        high, low = split(rights[at])
        right += [high, low, high]
    partial = dot(jnp.concatenate(right, axis=1), jnp.concatenate(left, axis=1), NT)
    for at in range(len(roots)):
        (mixed,) = times_blocks([roots[at]], delta_blocks)
        mixed_ref[at] = mixed * scales[at]
    half = rank // 2
    partial_ref[...] = jnp.concatenate([partial[:half], partial[half:]], axis=1)


def first_polar_kernel(after_ref, delta_ref, *refs):
    *gram_refs, mixed_ref, partial_ref, gram_ref = refs
    grams = [summed(gram_refs, at) for at in range(gram_ref.shape[0])]
    for at in range(len(grams)):
        gram_ref[at] = grams[at]
    delta = delta_ref[...]
    mix(*polar(grams, delta), delta, mixed_ref, partial_ref)


def later_polar_kernel(last, after_ref, delta_ref, change_ref, old_ref, *refs):
    if last:
        *cross_refs, mixed_ref, partial_ref = refs
    else:
        *cross_refs, mixed_ref, partial_ref, gram_ref = refs
    groups, rank, wide = old_ref.shape
    group = wide // rank
    mask = block_mask(rank, group)
    grams = []
    for at in range(groups):
        cross = summed(cross_refs, at)
        change = change_ref[at]
        (onward,) = times_blocks([change], block_diagonal(old_ref[at], mask, group))
        onward = cross[:, :wide] + 0.5 * onward
        (one,) = times_blocks([onward], block_diagonal(change, mask, group, NT), NT)
        (other,) = times_blocks([change], block_diagonal(onward, mask, group, NT), NT)
        grams.append(cross[:, wide:] + one + other)
        if not last:
            gram_ref[at] = grams[at]
    delta = delta_ref[...]
    mix(*polar(grams, delta), delta, mixed_ref, partial_ref)


def ahead_kernel(
    group, odd_ref, after_ref, inside_ref, near_ref, far_ref, target_ref, tall_ref, side_ref, rho_ref,
    inverse_ref, known_ref, cross_ref, *kept
):
    count, rank, rows = inside_ref.shape
    width = SWEEPS
    knowns, talls = [], []
    for k in range(count):
        aux = inside_ref[k]
        for at, mine, other in ((k, near_ref, far_ref), (k - count + width, far_ref, near_ref)):
            if 0 <= at < width:
                lanes = slice((at % 2) * rows, (at % 2 + 1) * rows)
                aux = aux + jnp.where(
                    odd_ref[0] == 1, mine[at // 2, :, lanes], other[at // 2, :, lanes]
                )
        target, tall = target_ref[k], tall_ref[k]
        if kept:
            aux_ref, dual_ref = kept
            aux_ref[k] = aux
            dual_ref[k] = target - aux
        known = dot(
            inverse_ref[k],
            right_triple(side_ref[k] + rho_ref[k : k + 1, 0:1] * (2.0 * aux - target - tall)),
        )
        known_ref[k] = known
        talls.append(tall)
        knowns.append(known + tall)
        if len(talls) == group:
            cross_ref[k // group] = jnp.concatenate(
                [cross_blocks(knowns, talls, rank), cross_blocks(knowns, knowns, rank)], axis=1
            )
            knowns, talls = [], []


def add_kernel(unread, *refs):
    *term_refs, total_ref = refs[unread:]
    total = term_refs[0][...]
    for ref in term_refs[1:]:
        total = total + ref[...]
    total_ref[...] = total


def new_delta(sum_refs, total, rank):
    packed = sum_refs[0][...]
    for ref in sum_refs[1:]:
        packed = packed + ref[...]
    packed = packed / total
    return jnp.concatenate([packed[:, :rank], packed[:, rank:]], axis=0)


def mixer_kernel(total, mixed_ref, inverse_ref, rho_ref, *refs):
    *sum_refs, delta_ref, change_ref, forward_ref = refs
    groups, rank, wide = mixed_ref.shape
    group = wide // rank
    turned = new_delta(sum_refs, total, rank)
    delta_ref[...] = turned.T
    mixers = from_left(turned, [mixed_ref[at] for at in range(groups)])
    place = lax.div(lax.broadcasted_iota(jnp.int32, (1, wide), 1), rank)
    for at in range(groups):
        mixer = mixers[at]
        slices = range(at * group, (at + 1) * group)
        inverses = jnp.concatenate([inverse_ref[k] for k in slices], axis=0)
        onward = diagonal_blocks(dot(inverses, right_triple(mixer)), rank, group)
        rho = rho_ref[at * group : at * group + 1, 0:1]
        for k in slices[1:]:
            rho = jnp.where(place == k - at * group, rho_ref[k : k + 1, 0:1], rho)
        forward = 2.0 * rho * onward
        forward_ref[at] = forward
        change_ref[at] = forward - mixer


def rows_kernel(odd_ref, aux_ref, before_ref, rho_ref, after_ref, *refs):
    (change_ref, forward_ref, tall_ref, known_ref, dual_ref) = refs[:5]
    (next_ref, target_ref, inside_ref, near_ref, far_ref) = refs[5:]
    targets = new_rows(change_ref, forward_ref, tall_ref, known_ref, next_ref)
    count = len(targets)
    for k in range(count):
        targets[k] = targets[k] + dual_ref[k]
        target_ref[k] = targets[k]
    rho = all_rho(before_ref, rho_ref, after_ref)
    smooth(
        odd_ref[0], [aux_ref[k] for k in range(count)], targets, rho,
        inside_ref, near_ref, far_ref,
    )


def last_rows_kernel(mixed_ref, change_ref, forward_ref, tall_ref, known_ref, *outs):
    mixed_tall_ref, evolving_ref, next_ref = outs
    evolvings = new_rows(change_ref, forward_ref, tall_ref, known_ref, next_ref)
    groups, rank, wide = mixed_ref.shape
    group = wide // rank
    for k in range(len(evolvings)):
        evolving_ref[k] = evolvings[k]
        place = (k % group) * rank
        mixed = left_triple(mixed_ref[k // group][:, place : place + rank])
        mixed_tall_ref[k] = right_triple(dot(mixed, right_triple(next_ref[k])))


def new_rows(change_ref, forward_ref, tall_ref, known_ref, next_ref):
    groups, rank, wide = change_ref.shape
    group = wide // rank
    evolvings = []
    for k in range(groups * group):
        lanes = slice((k % group) * rank, (k % group + 1) * rank)
        change, forward = change_ref[k // group][:, lanes], forward_ref[k // group][:, lanes]
        left = jnp.concatenate([left_triple(change), left_triple(forward)], axis=0)
        tall, known = tall_ref[k], known_ref[k]
        both = dot(left, right_triple(tall))
        next_ref[k] = known + tall + both[:rank]
        evolvings.append(known + both[rank:])
    return evolvings


def last_kernel(total, mixed_tall_ref, *refs):
    *sum_refs, coupled_ref, delta_ref = refs
    turned = new_delta(sum_refs, total, delta_ref.shape[0])
    delta_ref[...] = turned.T
    delta_left = left_triple(turned)
    for k in range(coupled_ref.shape[0]):
        coupled_ref[k] = dot(delta_left, mixed_tall_ref[k])


per_microsecond = 1_100_000_000


def call(
    kernel, name, outs, *args, scalars=0, unread=0, microseconds=0.3, limit=16, scratch=()
):
    flops = int(microseconds * per_microsecond)
    specs = [pl.BlockSpec(memory_space=pltpu.SMEM)] * scalars
    specs += [pl.BlockSpec(memory_space=pl.ANY)] * unread
    specs += [pl.BlockSpec(memory_space=pltpu.VMEM)] * (len(args) - len(specs))
    shapes = [jax.ShapeDtypeStruct(shape, dtype) for shape, dtype in outs]
    moved = sum(arg.size * arg.dtype.itemsize for arg in args)
    moved += sum(shape.size * shape.dtype.itemsize for shape in shapes)
    return pl.pallas_call(
        kernel,
        out_shape=shapes,
        in_specs=specs,
        out_specs=[pl.BlockSpec(memory_space=pltpu.VMEM)] * len(shapes),
        scratch_shapes=list(scratch),
        compiler_params=pltpu.CompilerParams(vmem_limit_bytes=limit * 1024 * 1024),
        cost_estimate=pl.CostEstimate(flops=flops, bytes_accessed=moved, transcendentals=0),
        name=name,
    )(*args)


def rotated(value, axis, shift):
    count = lax.axis_size(axis)
    return lax.ppermute(value, axis, [(i, (i + shift) % count) for i in range(count)])


def swapped(value, axis, first):
    count = lax.axis_size(axis)
    pairs = [((i + first) % count, (i + first + 1) % count) for i in range(0, count, 2)]
    return lax.ppermute(value, axis, pairs + [(b, a) for a, b in pairs])


def from_others(value, axis):
    return [rotated(value, axis, shift) for shift in range(1, lax.axis_size(axis))]


def stage_sizes(count):
    sizes = []
    while count > 1:
        sizes.append(next(size for size in (4, 2, 3, 5, 7, count) if count % size == 0))
        count //= sizes[-1]
    return sizes


def in_stages(value, axis, beside=None):
    count = lax.axis_size(axis)
    stride = 1
    terms, firsts = [value], []
    for size in stage_sizes(count):
        value = terms[0]
        if len(terms) > 1:
            unread = [] if beside is None else [beside]
            (value,) = call(
                functools.partial(add_kernel, len(unread)),
                "add",
                [(value.shape, f32)],
                *unread, *terms,
                unread=len(unread),
            )
        terms = [value]
        for shift in range(1, size):
            moves = []
            for i in range(count):
                digit = (i // stride) % size
                other = digit ^ shift if size in (2, 4) else (digit + shift) % size
                moves.append((i, i + (other - digit) * stride))
            terms.append(lax.ppermute(value, axis, moves))
        stride *= size
        firsts = firsts or terms
    return terms, firsts


def body(
    data, order, chan_factor, slice_weights, smooth_aux, coupled, smooth_dual, coupling_dual, delta
):
    count, all_rows, channels = data.shape
    rank = chan_factor.shape[1]
    rows = smooth_aux.shape[1]
    parts = lax.axis_size("chan")
    total = count * lax.axis_size("cuts")
    group = group_size(count, rank)
    groups = count // group
    wide = group * rank
    flip = lambda value: jnp.swapaxes(value, 1, 2)
    aux, coup, dual_s, dual_c = map(flip, (smooth_aux, coupled, smooth_dual, coupling_dual))
    factor = chan_factor.T
    state = ((count, rank, rows), f32)
    quads = ((groups, rank, wide), f32)
    square = ((rank, rank), f32)
    halo = (((SWEEPS + 1) // 2, rank, 2 * rows), f32)
    lanes = lambda height: ((height, 128), f32)
    scale = ((groups, 8, wide), f32)

    me = lax.axis_index("chan").astype(jnp.int32).reshape(1)
    odd = lax.rem(lax.axis_index("cuts"), 2).astype(jnp.int32).reshape(1)
    early = count // 4
    own, received = [], []
    for first, pairs, lead in ((0, early, True), (2 * early, count // 2 - early, False)):
        height = pairs * rows + (rank // 2 if lead else 0)
        projected = call(
            functools.partial(project_kernel, first, pairs, rows, lead),
            "project",
            [((height, 2 * rank), f32)] * parts + [(factor.shape, factor.dtype)] * lead,
            me, data, factor,
            scalars=1, unread=1, limit=52,
            scratch=[
                pltpu.VMEM((2 * pairs, all_rows, channels), data.dtype),
                pltpu.SemaphoreType.DMA((4 * pairs,)),
            ],
        )
        if lead:
            *projected, factor = projected
        own.append(projected[0])
        received.append([rotated(projected[shift], "chan", shift) for shift in range(1, parts)])

    late_weights, _ = lax.optimization_barrier((slice_weights, own[-1]))
    before = rotated(late_weights, "cuts", 1)
    after = rotated(late_weights, "cuts", -1)
    inverse, mover, rho, diagonal, columns, base = call(
        functools.partial(setup_kernel, parts, early * rows, group),
        "setup",
        [
            ((count, rank, 3 * rank), bf16),
            ((count // 2, 2 * rank, 6 * rank), bf16),
            lanes(count),
            ((count, rank), f32),
            ((rank, count), f32),
            state,
        ],
        order, own[0], *received[0], slice_weights, aux, coup, dual_s, dual_c,
        scalars=1,
    )
    half_state = ((early, 2 * rank, rows), f32)
    moved, turned = call(
        move_kernel, "move", [half_state, half_state], mover, own[0], *received[0]
    )
    tall, target, gram = call(
        functools.partial(first_kernel, group),
        "first",
        [state, state, quads],
        order, before, after, base, mover, dual_s, dual_c, moved, own[1], *received[1],
        scalars=1, unread=2,
        scratch=[pltpu.VMEM((count // 2, 2 * rank, rows), f32)],
    )
    side, before, after, inside, to_near, to_far = call(
        smooth_kernel,
        "smooth",
        [state, lanes(count), lanes(count), state, halo, halo],
        odd, order, aux, target, before, rho, after, diagonal, columns, turned, own[1],
        *received[1],
        scalars=2,
        scratch=[pltpu.VMEM((count // 2, 2 * rank, rows), f32)],
    )
    polar_outs = [quads, ((rank // 2, 2 * rank), f32), quads]
    for inner in range(INNER):
        if inner == 0:
            mixed, partial, gram = call(
                first_polar_kernel,
                "polar",
                polar_outs,
                inside, delta, gram, *from_others(gram, "chan"),
                unread=1, microseconds=3,
            )
        else:
            last = inner == INNER - 1
            mixed, partial, *gram = call(
                functools.partial(later_polar_kernel, last),
                "polar",
                polar_outs[:2] if last else polar_outs,
                inside, delta, change, old, cross, *crosses,
                unread=1,
            )
            gram = gram[0] if gram else None
        if inner == INNER - 1:
            mixed_tall, evolving = call(
                last_rows_kernel,
                "rows",
                [((count, 3 * rank, rows), bf16), state],
                mixed, change, forward, tall, known,
                scratch=[pltpu.VMEM(state[0], f32)],
            )
            coup, delta = call(
                functools.partial(last_kernel, total),
                "last",
                [state, square],
                mixed_tall, *in_stages(partial, "cuts")[0],
            )
            continue
        near = swapped(to_near, "cuts", 0)
        far = swapped(to_far, "cuts", 1)
        known, cross, *kept = call(
            functools.partial(ahead_kernel, group),
            "ahead",
            [state, ((groups, rank, 2 * wide), f32)] + [state] * (2 if inner < INNER - 2 else 0),
            odd, partial, inside, near, far, target, tall, side, rho, inverse,
            scalars=1, unread=1,
        )
        sums, firsts = in_stages(partial, "cuts", beside=cross)
        _, cross = lax.optimization_barrier((firsts, cross))
        crosses = from_others(cross, "chan")
        old = gram
        delta, change, forward = call(
            functools.partial(mixer_kernel, total),
            "mixer",
            [square, quads, quads],
            mixed, inverse, rho, *sums,
        )
        if inner < INNER - 2:
            tall, target, inside, to_near, to_far = call(
                rows_kernel,
                "rows",
                [state, state, state, halo, halo],
                odd, kept[0], before, rho, after, change, forward, tall, known, kept[1],
                scalars=1,
            )
    return (flip(evolving), flip(coup), delta)


def solution(mesh):
    return jax.shard_map(
        body,
        mesh=mesh,
        in_specs=(
            P("cuts", None, "chan"),
            P("cuts"),
            P("chan", None),
            P("cuts", None),
            P("cuts", "chan", None),
            P("cuts", "chan", None),
            P("cuts", "chan", None),
            P("cuts", "chan", None),
            P(),
        ),
        out_specs=(P("cuts", "chan", None), P("cuts", "chan", None), P()),
        check_vma=False,
    )
```

profile of v0, /device:TPU:0, one launch (start us, length us, event | category | flops | bytes accessed | tf_op | source)
XLA Modules:
  0.0 83.0 jit_solution(7249528372912151606)
XLA Ops:
  1.5 2.2 %project.2 = (f32[416,128]{1,0:T(8,128)S(1)}, f32[416,128]{1,0:T(8,128)S(1)}, bf16[64,512]{1,0:T(8,128)(2,1)S(1)}) custom-call(s32[1]{0:T(128)} %bitcast.2.me_ref, bf16[8,384,512]{2,1,0:T(8,128)(2,1)} %data_ref.3, bf16[64,512]{1,0:T(8,128)(2,1)S(1)} %bitcast.16), custom_call_target="tpu_custom_call" | custom-call | flops 330000000 | bytes 3702788 | tf_op jit(solution)/shard_map/project/pallas_call | solution.py:539
  3.7 3.0 %collective-permute-start.2 = (f32[416,128]{1,0:T(8,128)S(1)}, f32[416,128]{1,0:T(8,128)S(1)}, u32[]{:S(2)}, u32[]{:S(2)}) collective-permute-start(f32[416,128]{1,0:T(8,128)S(1)} %get-tuple-element.61), channel_id=1, source_target_pairs={{0,1},{1,0},{2,3},{3,2},{4,5},{5,4},{6,7},{7,6},{8,9},{9,8},{10,11... | collective-permute-start | bytes 638984 | tf_op jit(solution)/shard_map/ppermute | solution.py:553
  6.7 2.0 %project.3 = (f32[384,128]{1,0:T(8,128)S(1)}, f32[384,128]{1,0:T(8,128)S(1)}) custom-call(s32[1]{0:T(128)} %bitcast.2.me_ref, bf16[8,384,512]{2,1,0:T(8,128)(2,1)} %data_ref.3, bf16[64,512]{1,0:T(8,128)(2,1)S(1)} %get-tuple-element.57.factor_ref), custom_call_target="tpu_custom_call" | custom-call | flops 330000000 | bytes 3604484 | tf_op jit(solution)/shard_map/project/pallas_call | solution.py:539
  8.8 4.0 %collective-permute-start.1 = (f32[8,64]{1,0:T(8,128)S(1)}, f32[8,64]{1,0:T(8,128)S(1)}, u32[]{:S(2)}, u32[]{:S(2)}) collective-permute-start(f32[8,64]{1,0:T(8,128)S(1)} %copy-done.6), channel_id=1, source_target_pairs={{0,30},{2,0},{4,2},{6,4},{8,6},{10,8},{12,10},{14,12},{16,14},{18,... | collective-permute-start | bytes 6152 | tf_op jit(solution)/shard_map/ppermute | solution.py:553
  12.8 3.4 %setup.1 = (bf16[8,64,192]{2,1,0:T(8,128)(2,1)S(1)}, bf16[4,128,384]{2,1,0:T(8,128)(2,1)S(1)}, f32[8,128]{1,0:T(8,128)S(1)}, f32[8,64]{1,0:T(8,128)S(1)}, f32[64...) custom-call(s32[8]{0:T(128)S(1)} %copy-done.5, f32[416,128]{1,0:T(8,128)S(1)} %get-tuple-element.60.refs_0_, ...), custom_call_target="tpu_custom_call" | custom-call | flops 330000000 | bytes 2992160 | tf_op jit(solution)/shard_map/setup/pallas_call | solution.py:539
  16.5 2.0 %collective-permute-done.refs_0_.before_ref = f32[8,64]{1,0:T(8,128)S(1)} collective-permute-done((f32[8,64]{1,0:T(8,128)S(1)}, f32[8,64]{1,0:T(8,128)S(1)}, u32[]{:S(2)}, u32[]{:S(2)}) %collective-permute-start) | collective-permute-done | bytes 2080 | tf_op jit(solution)/shard_map/ppermute | solution.py:553
  18.5 1.2 %first.1 = (f32[8,64,192]{2,1,0:T(8,128)S(1)}, f32[8,64,192]{2,1,0:T(8,128)S(1)}, f32[4,64,128]{2,1,0:T(8,128)S(1)}) custom-call(s32[8]{0:T(128)S(1)} %copy-done.5, f32[8,64]{1,0:T(8,128)S(1)} %collective-permute-done.refs_0_.before_ref, f32[8,64]{1,0:T(8,128)S(1)} %collective-permute-done.1.refs_1_.after_ref, f32[8,64,192]{2,1,0:T(8,128)S(1)} %get-tuple-element.62.refs_2_, ...), custom_call_target="tpu_custom_call" | custom-call | flops 330000000 | bytes 3084320 | tf_op jit(solution)/shard_map/first/pallas_call | solution.py:539
  19.7 1.5 %collective-permute-start.4 = (f32[4,64,128]{2,1,0:T(8,128)S(1)}, f32[4,64,128]{2,1,0:T(8,128)S(1)}, u32[]{:S(2)}, u32[]{:S(2)}) collective-permute-start(f32[4,64,128]{2,1,0:T(8,128)S(1)} %get-tuple-element.72.refs_0_), channel_id=1, source_target_pairs={{0,1},{1,0},{2,3},{3,2},{4,5},{5,4},{6,7},{7,6},{8,9},{9,8},{10,11... | collective-permute-start | bytes 393224 | tf_op jit(solution)/shard_map/ppermute | solution.py:553
  21.3 1.2 %smooth.1 = (f32[8,64,192]{2,1,0:T(8,128)S(1)}, f32[8,128]{1,0:T(8,128)S(1)}, f32[8,128]{1,0:T(8,128)S(1)}, f32[8,64,192]{2,1,0:T(8,128)S(1)}, f32[2,64,384]{2,1,0:T(8,128)S(1)}, /*index=5*/f32[2,64,384]{2,1,0:T(8,128)S(1)}) custom-call(s32[1]{0:T(128)} %bitcast.odd_ref, s32[8]{0:T(128)S(1)} %copy-done.5, f32[8,64,192]{2,1,0:T(8,128)S(1)} %bitcast.10, ...), custom_call_target="tpu_custom_call" | custom-call | flops 330000000 | bytes 2576420 | tf_op jit(solution)/shard_map/smooth/pallas_call | solution.py:539
  22.5 3.3 %collective-permute-start.6 = (f32[2,64,384]{2,1,0:T(8,128)S(1)}, f32[2,64,384]{2,1,0:T(8,128)S(1)}, u32[]{:S(2)}, u32[]{:S(2)}) collective-permute-start(f32[2,64,384]{2,1,0:T(8,128)S(1)} %get-tuple-element.75), channel_id=1, source_target_pairs={{2,4},{6,8},{10,12},{14,16},{18,20},{22,24},{26,28},{30,0},{4,2},{... | collective-permute-start | bytes 589832 | tf_op jit(solution)/shard_map/ppermute | solution.py:559
  25.8 5.5 %polar.3 = (f32[4,64,128]{2,1,0:T(8,128)S(1)}, f32[32,128]{1,0:T(8,128)S(1)}, f32[4,64,128]{2,1,0:T(8,128)S(1)}) custom-call(f32[8,64,192]{2,1,0:T(8,128)S(1)} %get-tuple-element.71.after_ref.inside_ref, f32[64,64]{1,0:T(8,128)S(1)} %copy-done.7, f32[4,64,128]{2,1,0:T(8,128)S(1)} %get-tuple-element.72.refs_0_, f32[4,64,128]{2,1,0:T(8,128)S(1)} %collective-permute-done.4.refs_1_), custom_call_target="tpu_custom_call" | custom-call | flops 3300000000 | bytes 950272 | tf_op jit(solution)/shard_map/polar/pallas_call | solution.py:539
  31.4 1.8 %collective-permute-start.7 = (f32[32,128]{1,0:T(8,128)S(1)}, f32[32,128]{1,0:T(8,128)S(1)}, u32[]{:S(2)}, u32[]{:S(2)}) collective-permute-start(f32[32,128]{1,0:T(8,128)S(1)} %get-tuple-element.73.after_ref.refs_1_), channel_id=1, source_target_pairs={{0,2},{2,0},{4,6},{6,4},{8,10},{10,8},{12,14},{14,12},{16,18},{18,... | collective-permute-start | bytes 49160 | tf_op jit(solution)/shard_map/ppermute | solution.py:596
  33.2 1.2 %ahead.2 = (f32[8,64,192]{2,1,0:T(8,128)S(1)}, f32[4,64,256]{2,1,0:T(8,128)S(1)}, f32[8,64,192]{2,1,0:T(8,128)S(1)}, f32[8,64,192]{2,1,0:T(8,128)S(1)}) custom-call(s32[1]{0:T(128)} %bitcast.odd_ref, f32[32,128]{1,0:T(8,128)S(1)} %get-tuple-element.73.after_ref.refs_1_, f32[8,64,192]{2,1,0:T(8,128)S(1)} %get-tuple-element.71.after_ref.inside_ref, ...), custom_call_target="tpu_custom_call" | custom-call | flops 330000000 | bytes 3624964 | tf_op jit(solution)/shard_map/ahead/pallas_call | solution.py:539
  35.7 2.1 %collective-permute-start.12 = (f32[32,128]{1,0:T(8,128)S(1)}, f32[32,128]{1,0:T(8,128)S(1)}, u32[]{:S(2)}, u32[]{:S(2)}) collective-permute-start(f32[32,128]{1,0:T(8,128)S(1)} %add.3.refs_0_), channel_id=1, source_target_pairs={{0,24},{2,26},{4,28},{6,30},{8,16},{10,18},{12,20},{14,22},{16,8},... | collective-permute-start | bytes 49160 | tf_op jit(solution)/shard_map/ppermute | solution.py:596
  37.8 2.2 %collective-permute-start.10 = (f32[32,128]{1,0:T(8,128)S(1)}, f32[32,128]{1,0:T(8,128)S(1)}, u32[]{:S(2)}, u32[]{:S(2)}) collective-permute-start(f32[32,128]{1,0:T(8,128)S(1)} %add.3.refs_0_), channel_id=1, source_target_pairs={{0,8},{2,10},{4,12},{6,14},{8,0},{10,2},{12,4},{14,6},{16,24},{18,... | collective-permute-start | bytes 49160 | tf_op jit(solution)/shard_map/ppermute | solution.py:596
  40.1 1.1 %collective-permute-done.12.refs_3_ = f32[32,128]{1,0:T(8,128)S(1)} collective-permute-done((f32[32,128]{1,0:T(8,128)S(1)}, f32[32,128]{1,0:T(8,128)S(1)}, u32[]{:S(2)}, u32[]{:S(2)}) %collective-permute-start.12) | collective-permute-done | bytes 16416 | tf_op jit(solution)/shard_map/ppermute | solution.py:596
  41.2 1.2 %collective-permute-done.11.refs_2_ = f32[32,128]{1,0:T(8,128)S(1)} collective-permute-done((f32[32,128]{1,0:T(8,128)S(1)}, f32[32,128]{1,0:T(8,128)S(1)}, u32[]{:S(2)}, u32[]{:S(2)}) %collective-permute-start.11) | collective-permute-done | bytes 16416 | tf_op jit(solution)/shard_map/ppermute | solution.py:596
  43.8 2.7 %collective-permute-start.15 = (f32[2,64,384]{2,1,0:T(8,128)S(1)}, f32[2,64,384]{2,1,0:T(8,128)S(1)}, u32[]{:S(2)}, u32[]{:S(2)}) collective-permute-start(f32[2,64,384]{2,1,0:T(8,128)S(1)} %get-tuple-element.95), channel_id=1, source_target_pairs={{2,4},{6,8},{10,12},{14,16},{18,20},{22,24},{26,28},{30,0},{4,2},{... | collective-permute-start | bytes 589832 | tf_op jit(solution)/shard_map/ppermute | solution.py:559
  46.5 6.2 %polar.4 = (f32[4,64,128]{2,1,0:T(8,128)S(1)}, f32[32,128]{1,0:T(8,128)S(1)}, f32[4,64,128]{2,1,0:T(8,128)S(1)}) custom-call(f32[8,64,192]{2,1,0:T(8,128)S(1)} %get-tuple-element.88.after_ref.inside_ref, f32[64,64]{1,0:T(8,128)S(1)} %get-tuple-element.89.delta_ref, f32[4,64,128]{2,1,0:T(8,128)S(1)} %get-tuple-element.84.refs_0_.change_ref, ...), custom_call_target="tpu_custom_call" | custom-call | flops 330000000 | bytes 1474560 | tf_op jit(solution)/shard_map/polar/pallas_call | solution.py:539
  54.6 1.4 %ahead.3 = (f32[8,64,192]{2,1,0:T(8,128)S(1)}, f32[4,64,256]{2,1,0:T(8,128)S(1)}) custom-call(s32[1]{0:T(128)} %bitcast.odd_ref, f32[32,128]{1,0:T(8,128)S(1)} %get-tuple-element.93.after_ref.refs_1_, f32[8,64,192]{2,1,0:T(8,128)S(1)} %get-tuple-element.88.after_ref.inside_ref, f32[2,64,384]{2,1,0:T(8,128)S(1)} %collective-permute-done.14.near_ref, ...), custom_call_target="tpu_custom_call" | custom-call | flops 330000000 | bytes 2838532 | tf_op jit(solution)/shard_map/ahead/pallas_call | solution.py:539
  56.5 1.4 %collective-permute-start.22 = (f32[4,64,256]{2,1,0:T(8,128)S(1)}, f32[4,64,256]{2,1,0:T(8,128)S(1)}, u32[]{:S(2)}, u32[]{:S(2)}) collective-permute-start(f32[4,64,256]{2,1,0:T(8,128)S(1)} %get-tuple-element.102.refs_0_), channel_id=1, source_target_pairs={{0,1},{1,0},{2,3},{3,2},{4,5},{5,4},{6,7},{7,6},{8,9},{9,8},{10,11... | collective-permute-start | bytes 786440 | tf_op jit(solution)/shard_map/ppermute | solution.py:553
  57.9 2.1 %collective-permute-start.21 = (f32[32,128]{1,0:T(8,128)S(1)}, f32[32,128]{1,0:T(8,128)S(1)}, u32[]{:S(2)}, u32[]{:S(2)}) collective-permute-start(f32[32,128]{1,0:T(8,128)S(1)} %add.4.refs_0_), channel_id=1, source_target_pairs={{0,24},{2,26},{4,28},{6,30},{8,16},{10,18},{12,20},{14,22},{16,8},... | collective-permute-start | bytes 49160 | tf_op jit(solution)/shard_map/ppermute | solution.py:596
  60.2 2.1 %collective-permute-start.19 = (f32[32,128]{1,0:T(8,128)S(1)}, f32[32,128]{1,0:T(8,128)S(1)}, u32[]{:S(2)}, u32[]{:S(2)}) collective-permute-start(f32[32,128]{1,0:T(8,128)S(1)} %add.4.refs_0_), channel_id=1, source_target_pairs={{0,8},{2,10},{4,12},{6,14},{8,0},{10,2},{12,4},{14,6},{16,24},{18,... | collective-permute-start | bytes 49160 | tf_op jit(solution)/shard_map/ppermute | solution.py:596
  62.3 1.1 %collective-permute-done.21.refs_3_ = f32[32,128]{1,0:T(8,128)S(1)} collective-permute-done((f32[32,128]{1,0:T(8,128)S(1)}, f32[32,128]{1,0:T(8,128)S(1)}, u32[]{:S(2)}, u32[]{:S(2)}) %collective-permute-start.21) | collective-permute-done | bytes 16416 | tf_op jit(solution)/shard_map/ppermute | solution.py:596
  63.4 1.2 %collective-permute-done.20.refs_2_ = f32[32,128]{1,0:T(8,128)S(1)} collective-permute-done((f32[32,128]{1,0:T(8,128)S(1)}, f32[32,128]{1,0:T(8,128)S(1)}, u32[]{:S(2)}, u32[]{:S(2)}) %collective-permute-start.20) | collective-permute-done | bytes 16416 | tf_op jit(solution)/shard_map/ppermute | solution.py:596
  65.1 6.2 %polar.5 = (f32[4,64,128]{2,1,0:T(8,128)S(1)}, f32[32,128]{1,0:T(8,128)S(1)}) custom-call(f32[8,64,192]{2,1,0:T(8,128)S(1)} %get-tuple-element.88.after_ref.inside_ref, f32[64,64]{1,0:T(8,128)S(1)} %get-tuple-element.99.delta_ref, f32[4,64,128]{2,1,0:T(8,128)S(1)} %get-tuple-element.100.change_ref, f32[4,64,128]{2,1,0:T(8,128)S(1)} %get-tuple-element.101.old_ref, ...), custom_call_target="tpu_custom_call" | custom-call | flops 330000000 | bytes 1343488 | tf_op jit(solution)/shard_map/polar/pallas_call | solution.py:539
  71.9 1.2 %collective-permute-start.23 = (f32[32,128]{1,0:T(8,128)S(1)}, f32[32,128]{1,0:T(8,128)S(1)}, u32[]{:S(2)}, u32[]{:S(2)}) collective-permute-start(f32[32,128]{1,0:T(8,128)S(1)} %get-tuple-element.108.refs_0_), channel_id=1, source_target_pairs={{0,2},{2,0},{4,6},{6,4},{8,10},{10,8},{12,14},{14,12},{16,18},{18,... | collective-permute-start | bytes 49160 | tf_op jit(solution)/shard_map/ppermute | solution.py:596
  73.2 1.3 %collective-permute-done.25.refs_3_ = f32[32,128]{1,0:T(8,128)S(1)} collective-permute-done((f32[32,128]{1,0:T(8,128)S(1)}, f32[32,128]{1,0:T(8,128)S(1)}, u32[]{:S(2)}, u32[]{:S(2)}) %collective-permute-start.25) | collective-permute-done | bytes 16416 | tf_op jit(solution)/shard_map/ppermute | solution.py:596
  75.1 1.9 %collective-permute-start.28 = (f32[32,128]{1,0:T(8,128)S(1)}, f32[32,128]{1,0:T(8,128)S(1)}, u32[]{:S(2)}, u32[]{:S(2)}) collective-permute-start(f32[32,128]{1,0:T(8,128)S(1)} %add.5.refs_0_), channel_id=1, source_target_pairs={{0,24},{2,26},{4,28},{6,30},{8,16},{10,18},{12,20},{14,22},{16,8},... | collective-permute-start | bytes 49160 | tf_op jit(solution)/shard_map/ppermute | solution.py:596
  78.1 1.5 %collective-permute-start.26 = (f32[32,128]{1,0:T(8,128)S(1)}, f32[32,128]{1,0:T(8,128)S(1)}, u32[]{:S(2)}, u32[]{:S(2)}) collective-permute-start(f32[32,128]{1,0:T(8,128)S(1)} %add.5.refs_0_), channel_id=1, source_target_pairs={{0,8},{2,10},{4,12},{6,14},{8,0},{10,2},{12,4},{14,6},{16,24},{18,... | collective-permute-start | bytes 49160 | tf_op jit(solution)/shard_map/ppermute | solution.py:596
  79.6 1.2 %rows.3 = (bf16[8,192,192]{2,1,0:T(8,128)(2,1)S(1)}, f32[8,64,192]{2,1,0:T(8,128)}) custom-call(f32[4,64,128]{2,1,0:T(8,128)S(1)} %get-tuple-element.103.mixed_ref, f32[4,64,128]{2,1,0:T(8,128)S(1)} %get-tuple-element.100.change_ref, f32[4,64,128]{2,1,0:T(8,128)S(1)} %get-tuple-element.104.forward_ref, f32[8,64,192]{2,1,0:T(8,128)S(1)} %get-tuple-element.97.tall_ref, ...), custom_call_target="tpu_custom_call" | custom-call | flops 330000000 | bytes 2162688 | tf_op jit(solution)/shard_map/rows/pallas_call | solution.py:539
  81.9 1.1 %last.1 = (f32[8,64,192]{2,1,0:T(8,128)}, f32[64,64]{1,0:T(8,128)}) custom-call(bf16[8,192,192]{2,1,0:T(8,128)(2,1)S(1)} %get-tuple-element.107.mixed_tall_ref, f32[32,128]{1,0:T(8,128)S(1)} %add.5.refs_0_, f32[32,128]{1,0:T(8,128)S(1)} %collective-permute-done.26.refs_1_, f32[32,128]{1,0:T(8,128)S(1)} %collective-permute-done.27.refs_2_, ...), custom_call_target="tpu_custom_call" | custom-call | flops 330000000 | bytes 1064960 | tf_op jit(solution)/shard_map/last/pallas_call | solution.py:539
  (61 shorter events, 10.5 us)
Async XLA Ops:
  1.5 11.3 %copy-start.2 = (f32[8,192,64]{1,2,0:T(8,128)S(1)}, f32[8,192,64]{1,2,0:T(8,128)}, u32[]{:S(2)}) copy-start(f32[8,192,64]{1,2,0:T(8,128)} %param.16) | copy-start | bytes 1179652
  1.5 11.3 %copy-start.3 = (f32[8,192,64]{1,2,0:T(8,128)S(1)}, f32[8,192,64]{1,2,0:T(8,128)}, u32[]{:S(2)}) copy-start(f32[8,192,64]{1,2,0:T(8,128)} %param.14) | copy-start | bytes 1179652
  1.5 11.3 %copy-start.5 = (s32[8]{0:T(128)S(1)}, s32[8]{0:T(128)}, u32[]{:S(2)}) copy-start(s32[8]{0:T(128)} %order_ref.5) | copy-start | bytes 100
  3.7 9.1 %collective-permute-start.2 = (f32[416,128]{1,0:T(8,128)S(1)}, f32[416,128]{1,0:T(8,128)S(1)}, u32[]{:S(2)}, u32[]{:S(2)}) collective-permute-start(f32[416,128]{1,0:T(8,128)S(1)} %get-tuple-element.61), channel_id=1, source_target_pairs={{0,1},{1,0},{2,3},{3,2},{4,5},{5,4},{6,7},{7,6},{8,9},{9,8},{10,11... | collective-permute-start | bytes 638984 | tf_op jit(solution)/shard_map/ppermute | solution.py:553
  8.7 9.8 %collective-permute-start.3 = (f32[384,128]{1,0:T(8,128)S(1)}, f32[384,128]{1,0:T(8,128)S(1)}, u32[]{:S(2)}, u32[]{:S(2)}) collective-permute-start(f32[384,128]{1,0:T(8,128)S(1)} %get-tuple-element.65), channel_id=1, source_target_pairs={{0,1},{1,0},{2,3},{3,2},{4,5},{5,4},{6,7},{7,6},{8,9},{9,8},{10,11... | collective-permute-start | bytes 589832 | tf_op jit(solution)/shard_map/ppermute | solution.py:553
  8.8 7.7 %collective-permute-start.1 = (f32[8,64]{1,0:T(8,128)S(1)}, f32[8,64]{1,0:T(8,128)S(1)}, u32[]{:S(2)}, u32[]{:S(2)}) collective-permute-start(f32[8,64]{1,0:T(8,128)S(1)} %copy-done.6), channel_id=1, source_target_pairs={{0,30},{2,0},{4,2},{6,4},{8,6},{10,8},{12,10},{14,12},{16,14},{18,... | collective-permute-start | bytes 6152 | tf_op jit(solution)/shard_map/ppermute | solution.py:553
  12.8 5.7 %collective-permute-start = (f32[8,64]{1,0:T(8,128)S(1)}, f32[8,64]{1,0:T(8,128)S(1)}, u32[]{:S(2)}, u32[]{:S(2)}) collective-permute-start(f32[8,64]{1,0:T(8,128)S(1)} %copy-done.6), channel_id=1, source_target_pairs={{0,2},{2,4},{4,6},{6,8},{8,10},{10,12},{12,14},{14,16},{16,18},{18... | collective-permute-start | bytes 6152 | tf_op jit(solution)/shard_map/ppermute | solution.py:553
  19.7 6.1 %collective-permute-start.4 = (f32[4,64,128]{2,1,0:T(8,128)S(1)}, f32[4,64,128]{2,1,0:T(8,128)S(1)}, u32[]{:S(2)}, u32[]{:S(2)}) collective-permute-start(f32[4,64,128]{2,1,0:T(8,128)S(1)} %get-tuple-element.72.refs_0_), channel_id=1, source_target_pairs={{0,1},{1,0},{2,3},{3,2},{4,5},{5,4},{6,7},{7,6},{8,9},{9,8},{10,11... | collective-permute-start | bytes 393224 | tf_op jit(solution)/shard_map/ppermute | solution.py:553
  22.4 10.8 %collective-permute-start.5 = (f32[2,64,384]{2,1,0:T(8,128)S(1)}, f32[2,64,384]{2,1,0:T(8,128)S(1)}, u32[]{:S(2)}, u32[]{:S(2)}) collective-permute-start(f32[2,64,384]{2,1,0:T(8,128)S(1)} %get-tuple-element.74), channel_id=1, source_target_pairs={{0,2},{4,6},{8,10},{12,14},{16,18},{20,22},{24,26},{28,30},{2,0},{... | collective-permute-start | bytes 589832 | tf_op jit(solution)/shard_map/ppermute | solution.py:559
  22.5 10.7 %collective-permute-start.6 = (f32[2,64,384]{2,1,0:T(8,128)S(1)}, f32[2,64,384]{2,1,0:T(8,128)S(1)}, u32[]{:S(2)}, u32[]{:S(2)}) collective-permute-start(f32[2,64,384]{2,1,0:T(8,128)S(1)} %get-tuple-element.75), channel_id=1, source_target_pairs={{2,4},{6,8},{10,12},{14,16},{18,20},{22,24},{26,28},{30,0},{4,2},{... | collective-permute-start | bytes 589832 | tf_op jit(solution)/shard_map/ppermute | solution.py:559
  31.3 3.2 %collective-permute-start.9 = (f32[32,128]{1,0:T(8,128)S(1)}, f32[32,128]{1,0:T(8,128)S(1)}, u32[]{:S(2)}, u32[]{:S(2)}) collective-permute-start(f32[32,128]{1,0:T(8,128)S(1)} %get-tuple-element.73.after_ref.refs_1_), channel_id=1, source_target_pairs={{0,6},{2,4},{4,2},{6,0},{8,14},{10,12},{12,10},{14,8},{16,22},{18,... | collective-permute-start | bytes 49160 | tf_op jit(solution)/shard_map/ppermute | solution.py:596
  31.4 3.8 %collective-permute-start.8 = (f32[32,128]{1,0:T(8,128)S(1)}, f32[32,128]{1,0:T(8,128)S(1)}, u32[]{:S(2)}, u32[]{:S(2)}) collective-permute-start(f32[32,128]{1,0:T(8,128)S(1)} %get-tuple-element.73.after_ref.refs_1_), channel_id=1, source_target_pairs={{0,4},{2,6},{4,0},{6,2},{8,12},{10,14},{12,8},{14,10},{16,20},{18,... | collective-permute-start | bytes 49160 | tf_op jit(solution)/shard_map/ppermute | solution.py:596
  31.4 3.7 %collective-permute-start.7 = (f32[32,128]{1,0:T(8,128)S(1)}, f32[32,128]{1,0:T(8,128)S(1)}, u32[]{:S(2)}, u32[]{:S(2)}) collective-permute-start(f32[32,128]{1,0:T(8,128)S(1)} %get-tuple-element.73.after_ref.refs_1_), channel_id=1, source_target_pairs={{0,2},{2,0},{4,6},{6,4},{8,10},{10,8},{12,14},{14,12},{16,18},{18,... | collective-permute-start | bytes 49160 | tf_op jit(solution)/shard_map/ppermute | solution.py:596
  35.2 11.3 %collective-permute-start.13 = (f32[4,64,256]{2,1,0:T(8,128)S(1)}, f32[4,64,256]{2,1,0:T(8,128)S(1)}, u32[]{:S(2)}, u32[]{:S(2)}) collective-permute-start(f32[4,64,256]{2,1,0:T(8,128)S(1)} %get-tuple-element.91.refs_0_), channel_id=1, source_target_pairs={{0,1},{1,0},{2,3},{3,2},{4,5},{5,4},{6,7},{7,6},{8,9},{9,8},{10,11... | collective-permute-start | bytes 786440 | tf_op jit(solution)/shard_map/ppermute | solution.py:553
  35.7 5.5 %collective-permute-start.12 = (f32[32,128]{1,0:T(8,128)S(1)}, f32[32,128]{1,0:T(8,128)S(1)}, u32[]{:S(2)}, u32[]{:S(2)}) collective-permute-start(f32[32,128]{1,0:T(8,128)S(1)} %add.3.refs_0_), channel_id=1, source_target_pairs={{0,24},{2,26},{4,28},{6,30},{8,16},{10,18},{12,20},{14,22},{16,8},... | collective-permute-start | bytes 49160 | tf_op jit(solution)/shard_map/ppermute | solution.py:596
  37.8 4.6 %collective-permute-start.11 = (f32[32,128]{1,0:T(8,128)S(1)}, f32[32,128]{1,0:T(8,128)S(1)}, u32[]{:S(2)}, u32[]{:S(2)}) collective-permute-start(f32[32,128]{1,0:T(8,128)S(1)} %add.3.refs_0_), channel_id=1, source_target_pairs={{0,16},{2,18},{4,20},{6,22},{8,24},{10,26},{12,28},{14,30},{16,0},... | collective-permute-start | bytes 49160 | tf_op jit(solution)/shard_map/ppermute | solution.py:596
  37.8 4.6 %collective-permute-start.10 = (f32[32,128]{1,0:T(8,128)S(1)}, f32[32,128]{1,0:T(8,128)S(1)}, u32[]{:S(2)}, u32[]{:S(2)}) collective-permute-start(f32[32,128]{1,0:T(8,128)S(1)} %add.3.refs_0_), channel_id=1, source_target_pairs={{0,8},{2,10},{4,12},{6,14},{8,0},{10,2},{12,4},{14,6},{16,24},{18,... | collective-permute-start | bytes 49160 | tf_op jit(solution)/shard_map/ppermute | solution.py:596
  43.8 10.8 %collective-permute-start.14 = (f32[2,64,384]{2,1,0:T(8,128)S(1)}, f32[2,64,384]{2,1,0:T(8,128)S(1)}, u32[]{:S(2)}, u32[]{:S(2)}) collective-permute-start(f32[2,64,384]{2,1,0:T(8,128)S(1)} %get-tuple-element.94), channel_id=1, source_target_pairs={{0,2},{4,6},{8,10},{12,14},{16,18},{20,22},{24,26},{28,30},{2,0},{... | collective-permute-start | bytes 589832 | tf_op jit(solution)/shard_map/ppermute | solution.py:559
  43.8 10.7 %collective-permute-start.15 = (f32[2,64,384]{2,1,0:T(8,128)S(1)}, f32[2,64,384]{2,1,0:T(8,128)S(1)}, u32[]{:S(2)}, u32[]{:S(2)}) collective-permute-start(f32[2,64,384]{2,1,0:T(8,128)S(1)} %get-tuple-element.95), channel_id=1, source_target_pairs={{2,4},{6,8},{10,12},{14,16},{18,20},{22,24},{26,28},{30,0},{4,2},{... | collective-permute-start | bytes 589832 | tf_op jit(solution)/shard_map/ppermute | solution.py:559
  52.7 3.3 %collective-permute-start.18 = (f32[32,128]{1,0:T(8,128)S(1)}, f32[32,128]{1,0:T(8,128)S(1)}, u32[]{:S(2)}, u32[]{:S(2)}) collective-permute-start(f32[32,128]{1,0:T(8,128)S(1)} %get-tuple-element.93.after_ref.refs_1_), channel_id=1, source_target_pairs={{0,6},{2,4},{4,2},{6,0},{8,14},{10,12},{12,10},{14,8},{16,22},{18,... | collective-permute-start | bytes 49160 | tf_op jit(solution)/shard_map/ppermute | solution.py:596
  52.7 3.8 %collective-permute-start.17 = (f32[32,128]{1,0:T(8,128)S(1)}, f32[32,128]{1,0:T(8,128)S(1)}, u32[]{:S(2)}, u32[]{:S(2)}) collective-permute-start(f32[32,128]{1,0:T(8,128)S(1)} %get-tuple-element.93.after_ref.refs_1_), channel_id=1, source_target_pairs={{0,4},{2,6},{4,0},{6,2},{8,12},{10,14},{12,8},{14,10},{16,20},{18,... | collective-permute-start | bytes 49160 | tf_op jit(solution)/shard_map/ppermute | solution.py:596
  53.5 3.0 %collective-permute-start.16 = (f32[32,128]{1,0:T(8,128)S(1)}, f32[32,128]{1,0:T(8,128)S(1)}, u32[]{:S(2)}, u32[]{:S(2)}) collective-permute-start(f32[32,128]{1,0:T(8,128)S(1)} %get-tuple-element.93.after_ref.refs_1_), channel_id=1, source_target_pairs={{0,2},{2,0},{4,6},{6,4},{8,10},{10,8},{12,14},{14,12},{16,18},{18,... | collective-permute-start | bytes 49160 | tf_op jit(solution)/shard_map/ppermute | solution.py:596
  56.5 8.6 %collective-permute-start.22 = (f32[4,64,256]{2,1,0:T(8,128)S(1)}, f32[4,64,256]{2,1,0:T(8,128)S(1)}, u32[]{:S(2)}, u32[]{:S(2)}) collective-permute-start(f32[4,64,256]{2,1,0:T(8,128)S(1)} %get-tuple-element.102.refs_0_), channel_id=1, source_target_pairs={{0,1},{1,0},{2,3},{3,2},{4,5},{5,4},{6,7},{7,6},{8,9},{9,8},{10,11... | collective-permute-start | bytes 786440 | tf_op jit(solution)/shard_map/ppermute | solution.py:553
  57.9 5.5 %collective-permute-start.21 = (f32[32,128]{1,0:T(8,128)S(1)}, f32[32,128]{1,0:T(8,128)S(1)}, u32[]{:S(2)}, u32[]{:S(2)}) collective-permute-start(f32[32,128]{1,0:T(8,128)S(1)} %add.4.refs_0_), channel_id=1, source_target_pairs={{0,24},{2,26},{4,28},{6,30},{8,16},{10,18},{12,20},{14,22},{16,8},... | collective-permute-start | bytes 49160 | tf_op jit(solution)/shard_map/ppermute | solution.py:596
  60.0 4.6 %collective-permute-start.20 = (f32[32,128]{1,0:T(8,128)S(1)}, f32[32,128]{1,0:T(8,128)S(1)}, u32[]{:S(2)}, u32[]{:S(2)}) collective-permute-start(f32[32,128]{1,0:T(8,128)S(1)} %add.4.refs_0_), channel_id=1, source_target_pairs={{0,16},{2,18},{4,20},{6,22},{8,24},{10,26},{12,28},{14,30},{16,0},... | collective-permute-start | bytes 49160 | tf_op jit(solution)/shard_map/ppermute | solution.py:596
  60.2 4.4 %collective-permute-start.19 = (f32[32,128]{1,0:T(8,128)S(1)}, f32[32,128]{1,0:T(8,128)S(1)}, u32[]{:S(2)}, u32[]{:S(2)}) collective-permute-start(f32[32,128]{1,0:T(8,128)S(1)} %add.4.refs_0_), channel_id=1, source_target_pairs={{0,8},{2,10},{4,12},{6,14},{8,0},{10,2},{12,4},{14,6},{16,24},{18,... | collective-permute-start | bytes 49160 | tf_op jit(solution)/shard_map/ppermute | solution.py:596
  71.3 3.2 %collective-permute-start.25 = (f32[32,128]{1,0:T(8,128)S(1)}, f32[32,128]{1,0:T(8,128)S(1)}, u32[]{:S(2)}, u32[]{:S(2)}) collective-permute-start(f32[32,128]{1,0:T(8,128)S(1)} %get-tuple-element.108.refs_0_), channel_id=1, source_target_pairs={{0,6},{2,4},{4,2},{6,0},{8,14},{10,12},{12,10},{14,8},{16,22},{18,... | collective-permute-start | bytes 49160 | tf_op jit(solution)/shard_map/ppermute | solution.py:596
  71.3 3.8 %collective-permute-start.24 = (f32[32,128]{1,0:T(8,128)S(1)}, f32[32,128]{1,0:T(8,128)S(1)}, u32[]{:S(2)}, u32[]{:S(2)}) collective-permute-start(f32[32,128]{1,0:T(8,128)S(1)} %get-tuple-element.108.refs_0_), channel_id=1, source_target_pairs={{0,4},{2,6},{4,0},{6,2},{8,12},{10,14},{12,8},{14,10},{16,20},{18,... | collective-permute-start | bytes 49160 | tf_op jit(solution)/shard_map/ppermute | solution.py:596
  71.9 3.2 %collective-permute-start.23 = (f32[32,128]{1,0:T(8,128)S(1)}, f32[32,128]{1,0:T(8,128)S(1)}, u32[]{:S(2)}, u32[]{:S(2)}) collective-permute-start(f32[32,128]{1,0:T(8,128)S(1)} %get-tuple-element.108.refs_0_), channel_id=1, source_target_pairs={{0,2},{2,0},{4,6},{6,4},{8,10},{10,8},{12,14},{14,12},{16,18},{18,... | collective-permute-start | bytes 49160 | tf_op jit(solution)/shard_map/ppermute | solution.py:596
  75.1 5.7 %collective-permute-start.28 = (f32[32,128]{1,0:T(8,128)S(1)}, f32[32,128]{1,0:T(8,128)S(1)}, u32[]{:S(2)}, u32[]{:S(2)}) collective-permute-start(f32[32,128]{1,0:T(8,128)S(1)} %add.5.refs_0_), channel_id=1, source_target_pairs={{0,24},{2,26},{4,28},{6,30},{8,16},{10,18},{12,20},{14,22},{16,8},... | collective-permute-start | bytes 49160 | tf_op jit(solution)/shard_map/ppermute | solution.py:596
  77.0 4.6 %collective-permute-start.27 = (f32[32,128]{1,0:T(8,128)S(1)}, f32[32,128]{1,0:T(8,128)S(1)}, u32[]{:S(2)}, u32[]{:S(2)}) collective-permute-start(f32[32,128]{1,0:T(8,128)S(1)} %add.5.refs_0_), channel_id=1, source_target_pairs={{0,16},{2,18},{4,20},{6,22},{8,24},{10,26},{12,28},{14,30},{16,0},... | collective-permute-start | bytes 49160 | tf_op jit(solution)/shard_map/ppermute | solution.py:596
  78.1 3.8 %collective-permute-start.26 = (f32[32,128]{1,0:T(8,128)S(1)}, f32[32,128]{1,0:T(8,128)S(1)}, u32[]{:S(2)}, u32[]{:S(2)}) collective-permute-start(f32[32,128]{1,0:T(8,128)S(1)} %add.5.refs_0_), channel_id=1, source_target_pairs={{0,8},{2,10},{4,12},{6,14},{8,0},{10,2},{12,4},{14,6},{16,24},{18,... | collective-permute-start | bytes 49160 | tf_op jit(solution)/shard_map/ppermute | solution.py:596
  (5 other events, 40.4 us)
where the time goes:
time: 83.2 us; the launch traced here: 83 us
  starting transfers between devices  35.4 us (43%)
  Pallas kernels  34.9 us (42%)
  waiting for transfers between devices  10.9 us (13%)
  between operations  0.89 us (1%)
  local copies, waits for them, and re-layouts  0.86 us (1%)
    pallas_call x19, Pallas kernels, call(): pl.pallas_call(kernel, out_shape=shapes, in_specs=specs, out_specs=[pl.Bl...  34.9 us
    ppermute x18, starting transfers between devices, in_stages(): terms.append(lax.ppermute(value, axis, moves))  18.9 us
    ppermute x7, starting transfers between devices, rotated(): lax.ppermute(value, axis, [(i, (i + shift) % count) for i in range(count)])  10.5 us
    ppermute x18, waiting for transfers between devices, in_stages(): terms.append(lax.ppermute(value, axis, moves))  8.93 us
    ppermute x4, starting transfers between devices, swapped(): return lax.ppermute(value, axis, pairs + [(b, a) for a, b in pairs])  6.08 us
    ppermute x7, waiting for transfers between devices, rotated(): lax.ppermute(value, axis, [(i, (i + shift) % count) for i in range(count)])  1.99 us
  transfers between devices with their start and end apart: 29, of which 11 were waited for; matrix products, arithmetic and copies ran while one was open for 0% of the time, Pallas kernels for 29%

commit v1 on v0

--- a/solution.py
+++ b/solution.py
@@ -53,13 +53,21 @@
 
 
 def block_diagonal(value, mask, group, dims=NN):
-    high, low = [jnp.concatenate([part] * group, axis=0) * mask for part in split(value)]
-    return jnp.concatenate([high, low, high], axis=0 if dims == NN else 1)
+    high, low = split(value)
+    high = jnp.concatenate([high] * group, axis=0) * mask
+    low = jnp.concatenate([low] * group, axis=0) * mask
+    empty = jnp.zeros_like(high)
+    one, other = ([high, low], [high, empty]) if dims == NN else ([high, high], [low, empty])
+    return jnp.concatenate(
+        [jnp.concatenate(one, axis=1), jnp.concatenate(other, axis=1)], axis=0
+    )
 
 
 def times_blocks(values, blocks, dims=NN):
-    rank = values[0].shape[0]
-    total = dot(jnp.concatenate([left_triple(value) for value in values], axis=0), blocks, dims)
+    rank, wide = values[0].shape
+    left = [jnp.concatenate(split(value), axis=1) for value in values]
+    total = dot(jnp.concatenate(left, axis=0), blocks, dims)
+    total = total[:, :wide] + total[:, wide:]
     return [total[at * rank : (at + 1) * rank] for at in range(len(values))]
 
 
@@ -740,7 +748,7 @@
                 "rows",
                 [state, state, state, halo, halo],
                 odd, kept[0], before, rho, after, change, forward, tall, known, kept[1],
-                scalars=1,
+                scalars=1, microseconds=1,
             )
     return (flip(evolving), flip(coup), delta)
 

time: 83.2 us -> 76.4 us (0.918)
  Pallas kernels: 34.9 us -> 27.7 us
  waiting for transfers between devices: 10.9 us -> 12.8 us
  starting transfers between devices: 35.4 us -> 34 us
    pallas_call x19, Pallas kernels: 34.9 us -> 27.7 us  [call(): pl.pallas_call(kernel, out_shape=shapes, in_specs=specs, out_specs=[pl.Bl...]
    ppermute x7, waiting for transfers between devices: 1.99 us -> 3.97 us  [rotated(): lax.ppermute(value, axis, [(i, (i + shift) % count) for i in range(count)])]
    ppermute x4, starting transfers between devices: 6.08 us -> 4.34 us  [swapped(): return lax.ppermute(value, axis, pairs + [(b, a) for a, b in pairs])]
  transfers between devices with their start and end apart: 29 -> 29, of which waited for: 11 -> 13; matrix products, arithmetic and copies ran while one was open for 0% -> 0% of each run, Pallas kernels for 29% -> 25%
where the time goes in v1:
time: 76.4 us; the launch traced here: 76.2 us
  starting transfers between devices  34 us (45%)
  Pallas kernels  27.7 us (36%)
  waiting for transfers between devices  12.8 us (17%)
  between operations  0.88 us (1%)
  local copies, waits for them, and re-layouts  0.86 us (1%)
    pallas_call x19, Pallas kernels, call(): pl.pallas_call(kernel, out_shape=shapes, in_specs=specs, out_specs=[pl.Bl...  27.7 us
    ppermute x18, starting transfers between devices, in_stages(): terms.append(lax.ppermute(value, axis, moves))  19 us
    ppermute x7, starting transfers between devices, rotated(): lax.ppermute(value, axis, [(i, (i + shift) % count) for i in range(count)])  10.7 us
    ppermute x18, waiting for transfers between devices, in_stages(): terms.append(lax.ppermute(value, axis, moves))  8.82 us
    ppermute x4, starting transfers between devices, swapped(): return lax.ppermute(value, axis, pairs + [(b, a) for a, b in pairs])  4.34 us
    ppermute x7, waiting for transfers between devices, rotated(): lax.ppermute(value, axis, [(i, (i + shift) % count) for i in range(count)])  3.97 us
  transfers between devices with their start and end apart: 29, of which 13 were waited for; matrix products, arithmetic and copies ran while one was open for 0% of the time, Pallas kernels for 25%

profile of v1, /device:TPU:0, one launch (start us, length us, event | category | flops | bytes accessed | tf_op | source)
XLA Modules:
  0.0 76.2 jit_solution(13265349545913265367)
XLA Ops:
  1.5 2.2 %project.2 = (f32[416,128]{1,0:T(8,128)S(1)}, f32[416,128]{1,0:T(8,128)S(1)}, bf16[64,512]{1,0:T(8,128)(2,1)S(1)}) custom-call(s32[1]{0:T(128)} %bitcast.2.me_ref, bf16[8,384,512]{2,1,0:T(8,128)(2,1)} %data_ref.3, bf16[64,512]{1,0:T(8,128)(2,1)S(1)} %bitcast.16), custom_call_target="tpu_custom_call" | custom-call | flops 330000000 | bytes 3702788 | tf_op jit(solution)/shard_map/project/pallas_call | solution.py:547
  3.7 3.0 %collective-permute-start.2 = (f32[416,128]{1,0:T(8,128)S(1)}, f32[416,128]{1,0:T(8,128)S(1)}, u32[]{:S(2)}, u32[]{:S(2)}) collective-permute-start(f32[416,128]{1,0:T(8,128)S(1)} %get-tuple-element.61), channel_id=1, source_target_pairs={{0,1},{1,0},{2,3},{3,2},{4,5},{5,4},{6,7},{7,6},{8,9},{9,8},{10,11... | collective-permute-start | bytes 638984 | tf_op jit(solution)/shard_map/ppermute | solution.py:561
  6.7 2.0 %project.3 = (f32[384,128]{1,0:T(8,128)S(1)}, f32[384,128]{1,0:T(8,128)S(1)}) custom-call(s32[1]{0:T(128)} %bitcast.2.me_ref, bf16[8,384,512]{2,1,0:T(8,128)(2,1)} %data_ref.3, bf16[64,512]{1,0:T(8,128)(2,1)S(1)} %get-tuple-element.57.factor_ref), custom_call_target="tpu_custom_call" | custom-call | flops 330000000 | bytes 3604484 | tf_op jit(solution)/shard_map/project/pallas_call | solution.py:547
  8.8 4.0 %collective-permute-start.1 = (f32[8,64]{1,0:T(8,128)S(1)}, f32[8,64]{1,0:T(8,128)S(1)}, u32[]{:S(2)}, u32[]{:S(2)}) collective-permute-start(f32[8,64]{1,0:T(8,128)S(1)} %copy-done.6), channel_id=1, source_target_pairs={{0,30},{2,0},{4,2},{6,4},{8,6},{10,8},{12,10},{14,12},{16,14},{18,... | collective-permute-start | bytes 6152 | tf_op jit(solution)/shard_map/ppermute | solution.py:561
  12.8 2.8 %setup.1 = (bf16[8,64,192]{2,1,0:T(8,128)(2,1)S(1)}, bf16[4,128,384]{2,1,0:T(8,128)(2,1)S(1)}, f32[8,128]{1,0:T(8,128)S(1)}, f32[8,64]{1,0:T(8,128)S(1)}, f32[64...) custom-call(s32[8]{0:T(128)S(1)} %copy-done.5, f32[416,128]{1,0:T(8,128)S(1)} %get-tuple-element.60.refs_0_, ...), custom_call_target="tpu_custom_call" | custom-call | flops 330000000 | bytes 2992160 | tf_op jit(solution)/shard_map/setup/pallas_call | solution.py:547
  15.9 2.6 %collective-permute-done.refs_0_.before_ref = f32[8,64]{1,0:T(8,128)S(1)} collective-permute-done((f32[8,64]{1,0:T(8,128)S(1)}, f32[8,64]{1,0:T(8,128)S(1)}, u32[]{:S(2)}, u32[]{:S(2)}) %collective-permute-start) | collective-permute-done | bytes 2080 | tf_op jit(solution)/shard_map/ppermute | solution.py:561
  18.5 1.2 %first.1 = (f32[8,64,192]{2,1,0:T(8,128)S(1)}, f32[8,64,192]{2,1,0:T(8,128)S(1)}, f32[4,64,128]{2,1,0:T(8,128)S(1)}) custom-call(s32[8]{0:T(128)S(1)} %copy-done.5, f32[8,64]{1,0:T(8,128)S(1)} %collective-permute-done.refs_0_.before_ref, f32[8,64]{1,0:T(8,128)S(1)} %collective-permute-done.1.refs_1_.after_ref, f32[8,64,192]{2,1,0:T(8,128)S(1)} %get-tuple-element.62.refs_2_, ...), custom_call_target="tpu_custom_call" | custom-call | flops 330000000 | bytes 3084320 | tf_op jit(solution)/shard_map/first/pallas_call | solution.py:547
  19.7 1.5 %collective-permute-start.4 = (f32[4,64,128]{2,1,0:T(8,128)S(1)}, f32[4,64,128]{2,1,0:T(8,128)S(1)}, u32[]{:S(2)}, u32[]{:S(2)}) collective-permute-start(f32[4,64,128]{2,1,0:T(8,128)S(1)} %get-tuple-element.72.refs_0_), channel_id=1, source_target_pairs={{0,1},{1,0},{2,3},{3,2},{4,5},{5,4},{6,7},{7,6},{8,9},{9,8},{10,11... | collective-permute-start | bytes 393224 | tf_op jit(solution)/shard_map/ppermute | solution.py:561
  21.3 1.2 %smooth.1 = (f32[8,64,192]{2,1,0:T(8,128)S(1)}, f32[8,128]{1,0:T(8,128)S(1)}, f32[8,128]{1,0:T(8,128)S(1)}, f32[8,64,192]{2,1,0:T(8,128)S(1)}, f32[2,64,384]{2,1,0:T(8,128)S(1)}, /*index=5*/f32[2,64,384]{2,1,0:T(8,128)S(1)}) custom-call(s32[1]{0:T(128)} %bitcast.odd_ref, s32[8]{0:T(128)S(1)} %copy-done.5, f32[8,64,192]{2,1,0:T(8,128)S(1)} %bitcast.10, ...), custom_call_target="tpu_custom_call" | custom-call | flops 330000000 | bytes 2576420 | tf_op jit(solution)/shard_map/smooth/pallas_call | solution.py:547
  22.5 2.7 %collective-permute-start.6 = (f32[2,64,384]{2,1,0:T(8,128)S(1)}, f32[2,64,384]{2,1,0:T(8,128)S(1)}, u32[]{:S(2)}, u32[]{:S(2)}) collective-permute-start(f32[2,64,384]{2,1,0:T(8,128)S(1)} %get-tuple-element.75), channel_id=1, source_target_pairs={{2,4},{6,8},{10,12},{14,16},{18,20},{22,24},{26,28},{30,0},{4,2},{... | collective-permute-start | bytes 589832 | tf_op jit(solution)/shard_map/ppermute | solution.py:567
  25.2 3.4 %polar.3 = (f32[4,64,128]{2,1,0:T(8,128)S(1)}, f32[32,128]{1,0:T(8,128)S(1)}, f32[4,64,128]{2,1,0:T(8,128)S(1)}) custom-call(f32[8,64,192]{2,1,0:T(8,128)S(1)} %get-tuple-element.71.after_ref.inside_ref, f32[64,64]{1,0:T(8,128)S(1)} %copy-done.7, f32[4,64,128]{2,1,0:T(8,128)S(1)} %get-tuple-element.72.refs_0_, f32[4,64,128]{2,1,0:T(8,128)S(1)} %collective-permute-done.4.refs_1_), custom_call_target="tpu_custom_call" | custom-call | flops 3300000000 | bytes 950272 | tf_op jit(solution)/shard_map/polar/pallas_call | solution.py:547
  28.7 1.8 %collective-permute-start.7 = (f32[32,128]{1,0:T(8,128)S(1)}, f32[32,128]{1,0:T(8,128)S(1)}, u32[]{:S(2)}, u32[]{:S(2)}) collective-permute-start(f32[32,128]{1,0:T(8,128)S(1)} %get-tuple-element.73.after_ref.refs_1_), channel_id=1, source_target_pairs={{0,2},{2,0},{4,6},{6,4},{8,10},{10,8},{12,14},{14,12},{16,18},{18,... | collective-permute-start | bytes 49160 | tf_op jit(solution)/shard_map/ppermute | solution.py:604
  30.5 1.2 %ahead.2 = (f32[8,64,192]{2,1,0:T(8,128)S(1)}, f32[4,64,256]{2,1,0:T(8,128)S(1)}, f32[8,64,192]{2,1,0:T(8,128)S(1)}, f32[8,64,192]{2,1,0:T(8,128)S(1)}) custom-call(s32[1]{0:T(128)} %bitcast.odd_ref, f32[32,128]{1,0:T(8,128)S(1)} %get-tuple-element.73.after_ref.refs_1_, f32[8,64,192]{2,1,0:T(8,128)S(1)} %get-tuple-element.71.after_ref.inside_ref, ...), custom_call_target="tpu_custom_call" | custom-call | flops 330000000 | bytes 3624964 | tf_op jit(solution)/shard_map/ahead/pallas_call | solution.py:547
  32.5 2.4 %collective-permute-start.12 = (f32[32,128]{1,0:T(8,128)S(1)}, f32[32,128]{1,0:T(8,128)S(1)}, u32[]{:S(2)}, u32[]{:S(2)}) collective-permute-start(f32[32,128]{1,0:T(8,128)S(1)} %add.3.refs_0_), channel_id=1, source_target_pairs={{0,24},{2,26},{4,28},{6,30},{8,16},{10,18},{12,20},{14,22},{16,8},... | collective-permute-start | bytes 49160 | tf_op jit(solution)/shard_map/ppermute | solution.py:604
  34.9 2.0 %collective-permute-start.10 = (f32[32,128]{1,0:T(8,128)S(1)}, f32[32,128]{1,0:T(8,128)S(1)}, u32[]{:S(2)}, u32[]{:S(2)}) collective-permute-start(f32[32,128]{1,0:T(8,128)S(1)} %add.3.refs_0_), channel_id=1, source_target_pairs={{0,8},{2,10},{4,12},{6,14},{8,0},{10,2},{12,4},{14,6},{16,24},{18,... | collective-permute-start | bytes 49160 | tf_op jit(solution)/shard_map/ppermute | solution.py:604
  38.1 1.4 %collective-permute-done.11.refs_2_ = f32[32,128]{1,0:T(8,128)S(1)} collective-permute-done((f32[32,128]{1,0:T(8,128)S(1)}, f32[32,128]{1,0:T(8,128)S(1)}, u32[]{:S(2)}, u32[]{:S(2)}) %collective-permute-start.11) | collective-permute-done | bytes 16416 | tf_op jit(solution)/shard_map/ppermute | solution.py:604
  40.9 1.5 %collective-permute-start.15 = (f32[2,64,384]{2,1,0:T(8,128)S(1)}, f32[2,64,384]{2,1,0:T(8,128)S(1)}, u32[]{:S(2)}, u32[]{:S(2)}) collective-permute-start(f32[2,64,384]{2,1,0:T(8,128)S(1)} %get-tuple-element.95), channel_id=1, source_target_pairs={{2,4},{6,8},{10,12},{14,16},{18,20},{22,24},{26,28},{30,0},{4,2},{... | collective-permute-start | bytes 589832 | tf_op jit(solution)/shard_map/ppermute | solution.py:567
  42.4 1.4 %collective-permute-done.13.refs_1_ = f32[4,64,256]{2,1,0:T(8,128)S(1)} collective-permute-done((f32[4,64,256]{2,1,0:T(8,128)S(1)}, f32[4,64,256]{2,1,0:T(8,128)S(1)}, u32[]{:S(2)}, u32[]{:S(2)}) %collective-permute-start.13) | collective-permute-done | bytes 262176 | tf_op jit(solution)/shard_map/ppermute | solution.py:561
  43.8 3.9 %polar.4 = (f32[4,64,128]{2,1,0:T(8,128)S(1)}, f32[32,128]{1,0:T(8,128)S(1)}, f32[4,64,128]{2,1,0:T(8,128)S(1)}) custom-call(f32[8,64,192]{2,1,0:T(8,128)S(1)} %get-tuple-element.88.after_ref.inside_ref, f32[64,64]{1,0:T(8,128)S(1)} %get-tuple-element.89.delta_ref, f32[4,64,128]{2,1,0:T(8,128)S(1)} %get-tuple-element.84.refs_0_.change_ref, ...), custom_call_target="tpu_custom_call" | custom-call | flops 330000000 | bytes 1474560 | tf_op jit(solution)/shard_map/polar/pallas_call | solution.py:547
  47.9 1.4 %collective-permute-start.17 = (f32[32,128]{1,0:T(8,128)S(1)}, f32[32,128]{1,0:T(8,128)S(1)}, u32[]{:S(2)}, u32[]{:S(2)}) collective-permute-start(f32[32,128]{1,0:T(8,128)S(1)} %get-tuple-element.93.after_ref.refs_1_), channel_id=1, source_target_pairs={{0,4},{2,6},{4,0},{6,2},{8,12},{10,14},{12,8},{14,10},{16,20},{18,... | collective-permute-start | bytes 49160 | tf_op jit(solution)/shard_map/ppermute | solution.py:604
  49.6 1.4 %ahead.3 = (f32[8,64,192]{2,1,0:T(8,128)S(1)}, f32[4,64,256]{2,1,0:T(8,128)S(1)}) custom-call(s32[1]{0:T(128)} %bitcast.odd_ref, f32[32,128]{1,0:T(8,128)S(1)} %get-tuple-element.93.after_ref.refs_1_, f32[8,64,192]{2,1,0:T(8,128)S(1)} %get-tuple-element.88.after_ref.inside_ref, f32[2,64,384]{2,1,0:T(8,128)S(1)} %collective-permute-done.14.near_ref, ...), custom_call_target="tpu_custom_call" | custom-call | flops 330000000 | bytes 2838532 | tf_op jit(solution)/shard_map/ahead/pallas_call | solution.py:547
  52.7 2.6 %collective-permute-start.21 = (f32[32,128]{1,0:T(8,128)S(1)}, f32[32,128]{1,0:T(8,128)S(1)}, u32[]{:S(2)}, u32[]{:S(2)}) collective-permute-start(f32[32,128]{1,0:T(8,128)S(1)} %add.4.refs_0_), channel_id=1, source_target_pairs={{0,24},{2,26},{4,28},{6,30},{8,16},{10,18},{12,20},{14,22},{16,8},... | collective-permute-start | bytes 49160 | tf_op jit(solution)/shard_map/ppermute | solution.py:604
  55.3 1.8 %collective-permute-start.19 = (f32[32,128]{1,0:T(8,128)S(1)}, f32[32,128]{1,0:T(8,128)S(1)}, u32[]{:S(2)}, u32[]{:S(2)}) collective-permute-start(f32[32,128]{1,0:T(8,128)S(1)} %add.4.refs_0_), channel_id=1, source_target_pairs={{0,8},{2,10},{4,12},{6,14},{8,0},{10,2},{12,4},{14,6},{16,24},{18,... | collective-permute-start | bytes 49160 | tf_op jit(solution)/shard_map/ppermute | solution.py:604
  57.1 1.1 %collective-permute-done.21.refs_3_ = f32[32,128]{1,0:T(8,128)S(1)} collective-permute-done((f32[32,128]{1,0:T(8,128)S(1)}, f32[32,128]{1,0:T(8,128)S(1)}, u32[]{:S(2)}, u32[]{:S(2)}) %collective-permute-start.21) | collective-permute-done | bytes 16416 | tf_op jit(solution)/shard_map/ppermute | solution.py:604
  58.3 1.7 %collective-permute-done.20.refs_2_ = f32[32,128]{1,0:T(8,128)S(1)} collective-permute-done((f32[32,128]{1,0:T(8,128)S(1)}, f32[32,128]{1,0:T(8,128)S(1)}, u32[]{:S(2)}, u32[]{:S(2)}) %collective-permute-start.20) | collective-permute-done | bytes 16416 | tf_op jit(solution)/shard_map/ppermute | solution.py:604
  60.5 3.9 %polar.5 = (f32[4,64,128]{2,1,0:T(8,128)S(1)}, f32[32,128]{1,0:T(8,128)S(1)}) custom-call(f32[8,64,192]{2,1,0:T(8,128)S(1)} %get-tuple-element.88.after_ref.inside_ref, f32[64,64]{1,0:T(8,128)S(1)} %get-tuple-element.99.delta_ref, f32[4,64,128]{2,1,0:T(8,128)S(1)} %get-tuple-element.100.change_ref, f32[4,64,128]{2,1,0:T(8,128)S(1)} %get-tuple-element.101.old_ref, ...), custom_call_target="tpu_custom_call" | custom-call | flops 330000000 | bytes 1343488 | tf_op jit(solution)/shard_map/polar/pallas_call | solution.py:547
  65.2 1.1 %collective-permute-start.23 = (f32[32,128]{1,0:T(8,128)S(1)}, f32[32,128]{1,0:T(8,128)S(1)}, u32[]{:S(2)}, u32[]{:S(2)}) collective-permute-start(f32[32,128]{1,0:T(8,128)S(1)} %get-tuple-element.108.refs_0_), channel_id=1, source_target_pairs={{0,2},{2,0},{4,6},{6,4},{8,10},{10,8},{12,14},{14,12},{16,18},{18,... | collective-permute-start | bytes 49160 | tf_op jit(solution)/shard_map/ppermute | solution.py:604
  66.3 1.3 %collective-permute-done.25.refs_3_ = f32[32,128]{1,0:T(8,128)S(1)} collective-permute-done((f32[32,128]{1,0:T(8,128)S(1)}, f32[32,128]{1,0:T(8,128)S(1)}, u32[]{:S(2)}, u32[]{:S(2)}) %collective-permute-start.25) | collective-permute-done | bytes 16416 | tf_op jit(solution)/shard_map/ppermute | solution.py:604
  68.3 2.0 %collective-permute-start.28 = (f32[32,128]{1,0:T(8,128)S(1)}, f32[32,128]{1,0:T(8,128)S(1)}, u32[]{:S(2)}, u32[]{:S(2)}) collective-permute-start(f32[32,128]{1,0:T(8,128)S(1)} %add.5.refs_0_), channel_id=1, source_target_pairs={{0,24},{2,26},{4,28},{6,30},{8,16},{10,18},{12,20},{14,22},{16,8},... | collective-permute-start | bytes 49160 | tf_op jit(solution)/shard_map/ppermute | solution.py:604
  70.7 2.0 %collective-permute-start.26 = (f32[32,128]{1,0:T(8,128)S(1)}, f32[32,128]{1,0:T(8,128)S(1)}, u32[]{:S(2)}, u32[]{:S(2)}) collective-permute-start(f32[32,128]{1,0:T(8,128)S(1)} %add.5.refs_0_), channel_id=1, source_target_pairs={{0,8},{2,10},{4,12},{6,14},{8,0},{10,2},{12,4},{14,6},{16,24},{18,... | collective-permute-start | bytes 49160 | tf_op jit(solution)/shard_map/ppermute | solution.py:604
  72.7 1.2 %rows.3 = (bf16[8,192,192]{2,1,0:T(8,128)(2,1)S(1)}, f32[8,64,192]{2,1,0:T(8,128)}) custom-call(f32[4,64,128]{2,1,0:T(8,128)S(1)} %get-tuple-element.103.mixed_ref, f32[4,64,128]{2,1,0:T(8,128)S(1)} %get-tuple-element.100.change_ref, f32[4,64,128]{2,1,0:T(8,128)S(1)} %get-tuple-element.104.forward_ref, f32[8,64,192]{2,1,0:T(8,128)S(1)} %get-tuple-element.97.tall_ref, ...), custom_call_target="tpu_custom_call" | custom-call | flops 330000000 | bytes 2162688 | tf_op jit(solution)/shard_map/rows/pallas_call | solution.py:547
  75.1 1.1 %last.1 = (f32[8,64,192]{2,1,0:T(8,128)}, f32[64,64]{1,0:T(8,128)}) custom-call(bf16[8,192,192]{2,1,0:T(8,128)(2,1)S(1)} %get-tuple-element.107.mixed_tall_ref, f32[32,128]{1,0:T(8,128)S(1)} %add.5.refs_0_, f32[32,128]{1,0:T(8,128)S(1)} %collective-permute-done.26.refs_1_, f32[32,128]{1,0:T(8,128)S(1)} %collective-permute-done.27.refs_2_, ...), custom_call_target="tpu_custom_call" | custom-call | flops 330000000 | bytes 1064960 | tf_op jit(solution)/shard_map/last/pallas_call | solution.py:547
  (61 shorter events, 10.3 us)
Async XLA Ops:
  1.5 11.3 %copy-start.2 = (f32[8,192,64]{1,2,0:T(8,128)S(1)}, f32[8,192,64]{1,2,0:T(8,128)}, u32[]{:S(2)}) copy-start(f32[8,192,64]{1,2,0:T(8,128)} %param.16) | copy-start | bytes 1179652
  1.5 11.3 %copy-start.3 = (f32[8,192,64]{1,2,0:T(8,128)S(1)}, f32[8,192,64]{1,2,0:T(8,128)}, u32[]{:S(2)}) copy-start(f32[8,192,64]{1,2,0:T(8,128)} %param.14) | copy-start | bytes 1179652
  1.5 11.3 %copy-start.5 = (s32[8]{0:T(128)S(1)}, s32[8]{0:T(128)}, u32[]{:S(2)}) copy-start(s32[8]{0:T(128)} %order_ref.5) | copy-start | bytes 100
  3.7 9.1 %collective-permute-start.2 = (f32[416,128]{1,0:T(8,128)S(1)}, f32[416,128]{1,0:T(8,128)S(1)}, u32[]{:S(2)}, u32[]{:S(2)}) collective-permute-start(f32[416,128]{1,0:T(8,128)S(1)} %get-tuple-element.61), channel_id=1, source_target_pairs={{0,1},{1,0},{2,3},{3,2},{4,5},{5,4},{6,7},{7,6},{8,9},{9,8},{10,11... | collective-permute-start | bytes 638984 | tf_op jit(solution)/shard_map/ppermute | solution.py:561
  8.7 9.8 %collective-permute-start.3 = (f32[384,128]{1,0:T(8,128)S(1)}, f32[384,128]{1,0:T(8,128)S(1)}, u32[]{:S(2)}, u32[]{:S(2)}) collective-permute-start(f32[384,128]{1,0:T(8,128)S(1)} %get-tuple-element.65), channel_id=1, source_target_pairs={{0,1},{1,0},{2,3},{3,2},{4,5},{5,4},{6,7},{7,6},{8,9},{9,8},{10,11... | collective-permute-start | bytes 589832 | tf_op jit(solution)/shard_map/ppermute | solution.py:561
  8.8 7.1 %collective-permute-start.1 = (f32[8,64]{1,0:T(8,128)S(1)}, f32[8,64]{1,0:T(8,128)S(1)}, u32[]{:S(2)}, u32[]{:S(2)}) collective-permute-start(f32[8,64]{1,0:T(8,128)S(1)} %copy-done.6), channel_id=1, source_target_pairs={{0,30},{2,0},{4,2},{6,4},{8,6},{10,8},{12,10},{14,12},{16,14},{18,... | collective-permute-start | bytes 6152 | tf_op jit(solution)/shard_map/ppermute | solution.py:561
  12.8 5.7 %collective-permute-start = (f32[8,64]{1,0:T(8,128)S(1)}, f32[8,64]{1,0:T(8,128)S(1)}, u32[]{:S(2)}, u32[]{:S(2)}) collective-permute-start(f32[8,64]{1,0:T(8,128)S(1)} %copy-done.6), channel_id=1, source_target_pairs={{0,2},{2,4},{4,6},{6,8},{8,10},{10,12},{12,14},{14,16},{16,18},{18... | collective-permute-start | bytes 6152 | tf_op jit(solution)/shard_map/ppermute | solution.py:561
  19.7 5.4 %collective-permute-start.4 = (f32[4,64,128]{2,1,0:T(8,128)S(1)}, f32[4,64,128]{2,1,0:T(8,128)S(1)}, u32[]{:S(2)}, u32[]{:S(2)}) collective-permute-start(f32[4,64,128]{2,1,0:T(8,128)S(1)} %get-tuple-element.72.refs_0_), channel_id=1, source_target_pairs={{0,1},{1,0},{2,3},{3,2},{4,5},{5,4},{6,7},{7,6},{8,9},{9,8},{10,11... | collective-permute-start | bytes 393224 | tf_op jit(solution)/shard_map/ppermute | solution.py:561
  22.4 8.1 %collective-permute-start.5 = (f32[2,64,384]{2,1,0:T(8,128)S(1)}, f32[2,64,384]{2,1,0:T(8,128)S(1)}, u32[]{:S(2)}, u32[]{:S(2)}) collective-permute-start(f32[2,64,384]{2,1,0:T(8,128)S(1)} %get-tuple-element.74), channel_id=1, source_target_pairs={{0,2},{4,6},{8,10},{12,14},{16,18},{20,22},{24,26},{28,30},{2,0},{... | collective-permute-start | bytes 589832 | tf_op jit(solution)/shard_map/ppermute | solution.py:567
  22.5 8.0 %collective-permute-start.6 = (f32[2,64,384]{2,1,0:T(8,128)S(1)}, f32[2,64,384]{2,1,0:T(8,128)S(1)}, u32[]{:S(2)}, u32[]{:S(2)}) collective-permute-start(f32[2,64,384]{2,1,0:T(8,128)S(1)} %get-tuple-element.75), channel_id=1, source_target_pairs={{2,4},{6,8},{10,12},{14,16},{18,20},{22,24},{26,28},{30,0},{4,2},{... | collective-permute-start | bytes 589832 | tf_op jit(solution)/shard_map/ppermute | solution.py:567
  28.6 3.2 %collective-permute-start.9 = (f32[32,128]{1,0:T(8,128)S(1)}, f32[32,128]{1,0:T(8,128)S(1)}, u32[]{:S(2)}, u32[]{:S(2)}) collective-permute-start(f32[32,128]{1,0:T(8,128)S(1)} %get-tuple-element.73.after_ref.refs_1_), channel_id=1, source_target_pairs={{0,6},{2,4},{4,2},{6,0},{8,14},{10,12},{12,10},{14,8},{16,22},{18,... | collective-permute-start | bytes 49160 | tf_op jit(solution)/shard_map/ppermute | solution.py:604
  28.7 3.8 %collective-permute-start.8 = (f32[32,128]{1,0:T(8,128)S(1)}, f32[32,128]{1,0:T(8,128)S(1)}, u32[]{:S(2)}, u32[]{:S(2)}) collective-permute-start(f32[32,128]{1,0:T(8,128)S(1)} %get-tuple-element.73.after_ref.refs_1_), channel_id=1, source_target_pairs={{0,4},{2,6},{4,0},{6,2},{8,12},{10,14},{12,8},{14,10},{16,20},{18,... | collective-permute-start | bytes 49160 | tf_op jit(solution)/shard_map/ppermute | solution.py:604
  28.7 3.7 %collective-permute-start.7 = (f32[32,128]{1,0:T(8,128)S(1)}, f32[32,128]{1,0:T(8,128)S(1)}, u32[]{:S(2)}, u32[]{:S(2)}) collective-permute-start(f32[32,128]{1,0:T(8,128)S(1)} %get-tuple-element.73.after_ref.refs_1_), channel_id=1, source_target_pairs={{0,2},{2,0},{4,6},{6,4},{8,10},{10,8},{12,14},{14,12},{16,18},{18,... | collective-permute-start | bytes 49160 | tf_op jit(solution)/shard_map/ppermute | solution.py:604
  32.5 5.6 %collective-permute-start.12 = (f32[32,128]{1,0:T(8,128)S(1)}, f32[32,128]{1,0:T(8,128)S(1)}, u32[]{:S(2)}, u32[]{:S(2)}) collective-permute-start(f32[32,128]{1,0:T(8,128)S(1)} %add.3.refs_0_), channel_id=1, source_target_pairs={{0,24},{2,26},{4,28},{6,30},{8,16},{10,18},{12,20},{14,22},{16,8},... | collective-permute-start | bytes 49160 | tf_op jit(solution)/shard_map/ppermute | solution.py:604
  34.9 4.6 %collective-permute-start.11 = (f32[32,128]{1,0:T(8,128)S(1)}, f32[32,128]{1,0:T(8,128)S(1)}, u32[]{:S(2)}, u32[]{:S(2)}) collective-permute-start(f32[32,128]{1,0:T(8,128)S(1)} %add.3.refs_0_), channel_id=1, source_target_pairs={{0,16},{2,18},{4,20},{6,22},{8,24},{10,26},{12,28},{14,30},{16,0},... | collective-permute-start | bytes 49160 | tf_op jit(solution)/shard_map/ppermute | solution.py:604
  34.9 4.6 %collective-permute-start.10 = (f32[32,128]{1,0:T(8,128)S(1)}, f32[32,128]{1,0:T(8,128)S(1)}, u32[]{:S(2)}, u32[]{:S(2)}) collective-permute-start(f32[32,128]{1,0:T(8,128)S(1)} %add.3.refs_0_), channel_id=1, source_target_pairs={{0,8},{2,10},{4,12},{6,14},{8,0},{10,2},{12,4},{14,6},{16,24},{18,... | collective-permute-start | bytes 49160 | tf_op jit(solution)/shard_map/ppermute | solution.py:604
  36.9 6.8 %collective-permute-start.13 = (f32[4,64,256]{2,1,0:T(8,128)S(1)}, f32[4,64,256]{2,1,0:T(8,128)S(1)}, u32[]{:S(2)}, u32[]{:S(2)}) collective-permute-start(f32[4,64,256]{2,1,0:T(8,128)S(1)} %get-tuple-element.91.refs_0_), channel_id=1, source_target_pairs={{0,1},{1,0},{2,3},{3,2},{4,5},{5,4},{6,7},{7,6},{8,9},{9,8},{10,11... | collective-permute-start | bytes 786440 | tf_op jit(solution)/shard_map/ppermute | solution.py:561
  40.8 8.8 %collective-permute-start.14 = (f32[2,64,384]{2,1,0:T(8,128)S(1)}, f32[2,64,384]{2,1,0:T(8,128)S(1)}, u32[]{:S(2)}, u32[]{:S(2)}) collective-permute-start(f32[2,64,384]{2,1,0:T(8,128)S(1)} %get-tuple-element.94), channel_id=1, source_target_pairs={{0,2},{4,6},{8,10},{12,14},{16,18},{20,22},{24,26},{28,30},{2,0},{... | collective-permute-start | bytes 589832 | tf_op jit(solution)/shard_map/ppermute | solution.py:567
  40.9 8.7 %collective-permute-start.15 = (f32[2,64,384]{2,1,0:T(8,128)S(1)}, f32[2,64,384]{2,1,0:T(8,128)S(1)}, u32[]{:S(2)}, u32[]{:S(2)}) collective-permute-start(f32[2,64,384]{2,1,0:T(8,128)S(1)} %get-tuple-element.95), channel_id=1, source_target_pairs={{2,4},{6,8},{10,12},{14,16},{18,20},{22,24},{26,28},{30,0},{4,2},{... | collective-permute-start | bytes 589832 | tf_op jit(solution)/shard_map/ppermute | solution.py:567
  47.7 3.4 %collective-permute-start.18 = (f32[32,128]{1,0:T(8,128)S(1)}, f32[32,128]{1,0:T(8,128)S(1)}, u32[]{:S(2)}, u32[]{:S(2)}) collective-permute-start(f32[32,128]{1,0:T(8,128)S(1)} %get-tuple-element.93.after_ref.refs_1_), channel_id=1, source_target_pairs={{0,6},{2,4},{4,2},{6,0},{8,14},{10,12},{12,10},{14,8},{16,22},{18,... | collective-permute-start | bytes 49160 | tf_op jit(solution)/shard_map/ppermute | solution.py:604
  47.9 3.7 %collective-permute-start.17 = (f32[32,128]{1,0:T(8,128)S(1)}, f32[32,128]{1,0:T(8,128)S(1)}, u32[]{:S(2)}, u32[]{:S(2)}) collective-permute-start(f32[32,128]{1,0:T(8,128)S(1)} %get-tuple-element.93.after_ref.refs_1_), channel_id=1, source_target_pairs={{0,4},{2,6},{4,0},{6,2},{8,12},{10,14},{12,8},{14,10},{16,20},{18,... | collective-permute-start | bytes 49160 | tf_op jit(solution)/shard_map/ppermute | solution.py:604
  49.3 2.4 %collective-permute-start.16 = (f32[32,128]{1,0:T(8,128)S(1)}, f32[32,128]{1,0:T(8,128)S(1)}, u32[]{:S(2)}, u32[]{:S(2)}) collective-permute-start(f32[32,128]{1,0:T(8,128)S(1)} %get-tuple-element.93.after_ref.refs_1_), channel_id=1, source_target_pairs={{0,2},{2,0},{4,6},{6,4},{8,10},{10,8},{12,14},{14,12},{16,18},{18,... | collective-permute-start | bytes 49160 | tf_op jit(solution)/shard_map/ppermute | solution.py:604
  51.6 8.8 %collective-permute-start.22 = (f32[4,64,256]{2,1,0:T(8,128)S(1)}, f32[4,64,256]{2,1,0:T(8,128)S(1)}, u32[]{:S(2)}, u32[]{:S(2)}) collective-permute-start(f32[4,64,256]{2,1,0:T(8,128)S(1)} %get-tuple-element.102.refs_0_), channel_id=1, source_target_pairs={{0,1},{1,0},{2,3},{3,2},{4,5},{5,4},{6,7},{7,6},{8,9},{9,8},{10,11... | collective-permute-start | bytes 786440 | tf_op jit(solution)/shard_map/ppermute | solution.py:561
  52.7 5.5 %collective-permute-start.21 = (f32[32,128]{1,0:T(8,128)S(1)}, f32[32,128]{1,0:T(8,128)S(1)}, u32[]{:S(2)}, u32[]{:S(2)}) collective-permute-start(f32[32,128]{1,0:T(8,128)S(1)} %add.4.refs_0_), channel_id=1, source_target_pairs={{0,24},{2,26},{4,28},{6,30},{8,16},{10,18},{12,20},{14,22},{16,8},... | collective-permute-start | bytes 49160 | tf_op jit(solution)/shard_map/ppermute | solution.py:604
  55.3 4.6 %collective-permute-start.20 = (f32[32,128]{1,0:T(8,128)S(1)}, f32[32,128]{1,0:T(8,128)S(1)}, u32[]{:S(2)}, u32[]{:S(2)}) collective-permute-start(f32[32,128]{1,0:T(8,128)S(1)} %add.4.refs_0_), channel_id=1, source_target_pairs={{0,16},{2,18},{4,20},{6,22},{8,24},{10,26},{12,28},{14,30},{16,0},... | collective-permute-start | bytes 49160 | tf_op jit(solution)/shard_map/ppermute | solution.py:604
  55.3 4.6 %collective-permute-start.19 = (f32[32,128]{1,0:T(8,128)S(1)}, f32[32,128]{1,0:T(8,128)S(1)}, u32[]{:S(2)}, u32[]{:S(2)}) collective-permute-start(f32[32,128]{1,0:T(8,128)S(1)} %add.4.refs_0_), channel_id=1, source_target_pairs={{0,8},{2,10},{4,12},{6,14},{8,0},{10,2},{12,4},{14,6},{16,24},{18,... | collective-permute-start | bytes 49160 | tf_op jit(solution)/shard_map/ppermute | solution.py:604
  64.4 3.2 %collective-permute-start.25 = (f32[32,128]{1,0:T(8,128)S(1)}, f32[32,128]{1,0:T(8,128)S(1)}, u32[]{:S(2)}, u32[]{:S(2)}) collective-permute-start(f32[32,128]{1,0:T(8,128)S(1)} %get-tuple-element.108.refs_0_), channel_id=1, source_target_pairs={{0,6},{2,4},{4,2},{6,0},{8,14},{10,12},{12,10},{14,8},{16,22},{18,... | collective-permute-start | bytes 49160 | tf_op jit(solution)/shard_map/ppermute | solution.py:604
  64.4 3.8 %collective-permute-start.24 = (f32[32,128]{1,0:T(8,128)S(1)}, f32[32,128]{1,0:T(8,128)S(1)}, u32[]{:S(2)}, u32[]{:S(2)}) collective-permute-start(f32[32,128]{1,0:T(8,128)S(1)} %get-tuple-element.108.refs_0_), channel_id=1, source_target_pairs={{0,4},{2,6},{4,0},{6,2},{8,12},{10,14},{12,8},{14,10},{16,20},{18,... | collective-permute-start | bytes 49160 | tf_op jit(solution)/shard_map/ppermute | solution.py:604
  65.2 3.1 %collective-permute-start.23 = (f32[32,128]{1,0:T(8,128)S(1)}, f32[32,128]{1,0:T(8,128)S(1)}, u32[]{:S(2)}, u32[]{:S(2)}) collective-permute-start(f32[32,128]{1,0:T(8,128)S(1)} %get-tuple-element.108.refs_0_), channel_id=1, source_target_pairs={{0,2},{2,0},{4,6},{6,4},{8,10},{10,8},{12,14},{14,12},{16,18},{18,... | collective-permute-start | bytes 49160 | tf_op jit(solution)/shard_map/ppermute | solution.py:604
  68.3 5.7 %collective-permute-start.28 = (f32[32,128]{1,0:T(8,128)S(1)}, f32[32,128]{1,0:T(8,128)S(1)}, u32[]{:S(2)}, u32[]{:S(2)}) collective-permute-start(f32[32,128]{1,0:T(8,128)S(1)} %add.5.refs_0_), channel_id=1, source_target_pairs={{0,24},{2,26},{4,28},{6,30},{8,16},{10,18},{12,20},{14,22},{16,8},... | collective-permute-start | bytes 49160 | tf_op jit(solution)/shard_map/ppermute | solution.py:604
  70.3 4.8 %collective-permute-start.27 = (f32[32,128]{1,0:T(8,128)S(1)}, f32[32,128]{1,0:T(8,128)S(1)}, u32[]{:S(2)}, u32[]{:S(2)}) collective-permute-start(f32[32,128]{1,0:T(8,128)S(1)} %add.5.refs_0_), channel_id=1, source_target_pairs={{0,16},{2,18},{4,20},{6,22},{8,24},{10,26},{12,28},{14,30},{16,0},... | collective-permute-start | bytes 49160 | tf_op jit(solution)/shard_map/ppermute | solution.py:604
  70.7 4.4 %collective-permute-start.26 = (f32[32,128]{1,0:T(8,128)S(1)}, f32[32,128]{1,0:T(8,128)S(1)}, u32[]{:S(2)}, u32[]{:S(2)}) collective-permute-start(f32[32,128]{1,0:T(8,128)S(1)} %add.5.refs_0_), channel_id=1, source_target_pairs={{0,8},{2,10},{4,12},{6,14},{8,0},{10,2},{12,4},{14,6},{16,24},{18,... | collective-permute-start | bytes 49160 | tf_op jit(solution)/shard_map/ppermute | solution.py:604
  (5 other events, 40.4 us)

commit v2 on v1

--- a/solution.py
+++ b/solution.py
@@ -748,7 +748,7 @@
                 "rows",
                 [state, state, state, halo, halo],
                 odd, kept[0], before, rho, after, change, forward, tall, known, kept[1],
-                scalars=1, microseconds=1,
+                scalars=1,
             )
     return (flip(evolving), flip(coup), delta)
 

time: 76.4 us -> 76.3 us (level)
  waiting for transfers between devices: 12.8 us -> 11.9 us
  starting transfers between devices: 34 us -> 34.8 us
    ppermute x7, waiting for transfers between devices: 3.97 us -> 2.61 us  [rotated(): lax.ppermute(value, axis, [(i, (i + shift) % count) for i in range(count)])]
    ppermute x4, starting transfers between devices: 4.34 us -> 5.23 us  [swapped(): return lax.ppermute(value, axis, pairs + [(b, a) for a, b in pairs])]
  transfers between devices with their start and end apart: 29 -> 29, of which waited for: 13 -> 12; matrix products, arithmetic and copies ran while one was open for 0% -> 0% of each run, Pallas kernels for 25% -> 25%
where the time goes in v2:
time: 76.3 us; the launch traced here: 76.1 us
  starting transfers between devices  34.8 us (46%)
  Pallas kernels  27.7 us (36%)
  waiting for transfers between devices  11.9 us (16%)
  between operations  0.89 us (1%)
  local copies, waits for them, and re-layouts  0.86 us (1%)
    pallas_call x19, Pallas kernels, call(): pl.pallas_call(kernel, out_shape=shapes, in_specs=specs, out_specs=[pl.Bl...  27.7 us
    ppermute x18, starting transfers between devices, in_stages(): terms.append(lax.ppermute(value, axis, moves))  18.9 us
    ppermute x7, starting transfers between devices, rotated(): lax.ppermute(value, axis, [(i, (i + shift) % count) for i in range(count)])  10.6 us
    ppermute x18, waiting for transfers between devices, in_stages(): terms.append(lax.ppermute(value, axis, moves))  9.26 us
    ppermute x4, starting transfers between devices, swapped(): return lax.ppermute(value, axis, pairs + [(b, a) for a, b in pairs])  5.23 us
    ppermute x7, waiting for transfers between devices, rotated(): lax.ppermute(value, axis, [(i, (i + shift) % count) for i in range(count)])  2.61 us
  transfers between devices with their start and end apart: 29, of which 12 were waited for; matrix products, arithmetic and copies ran while one was open for 0% of the time, Pallas kernels for 25%

profile of v2, /device:TPU:0, one launch (start us, length us, event | category | flops | bytes accessed | tf_op | source)
XLA Modules:
  0.0 76.1 jit_solution(5841031786453799855)
XLA Ops:
  1.5 2.2 %project.2 = (f32[416,128]{1,0:T(8,128)S(1)}, f32[416,128]{1,0:T(8,128)S(1)}, bf16[64,512]{1,0:T(8,128)(2,1)S(1)}) custom-call(s32[1]{0:T(128)} %bitcast.2.me_ref, bf16[8,384,512]{2,1,0:T(8,128)(2,1)} %data_ref.3, bf16[64,512]{1,0:T(8,128)(2,1)S(1)} %bitcast.16), custom_call_target="tpu_custom_call" | custom-call | flops 330000000 | bytes 3702788 | tf_op jit(solution)/shard_map/project/pallas_call | solution.py:547
  3.7 3.0 %collective-permute-start.2 = (f32[416,128]{1,0:T(8,128)S(1)}, f32[416,128]{1,0:T(8,128)S(1)}, u32[]{:S(2)}, u32[]{:S(2)}) collective-permute-start(f32[416,128]{1,0:T(8,128)S(1)} %get-tuple-element.61), channel_id=1, source_target_pairs={{0,1},{1,0},{2,3},{3,2},{4,5},{5,4},{6,7},{7,6},{8,9},{9,8},{10,11... | collective-permute-start | bytes 638984 | tf_op jit(solution)/shard_map/ppermute | solution.py:561
  6.7 2.0 %project.3 = (f32[384,128]{1,0:T(8,128)S(1)}, f32[384,128]{1,0:T(8,128)S(1)}) custom-call(s32[1]{0:T(128)} %bitcast.2.me_ref, bf16[8,384,512]{2,1,0:T(8,128)(2,1)} %data_ref.3, bf16[64,512]{1,0:T(8,128)(2,1)S(1)} %get-tuple-element.57.factor_ref), custom_call_target="tpu_custom_call" | custom-call | flops 330000000 | bytes 3604484 | tf_op jit(solution)/shard_map/project/pallas_call | solution.py:547
  8.8 4.0 %collective-permute-start.1 = (f32[8,64]{1,0:T(8,128)S(1)}, f32[8,64]{1,0:T(8,128)S(1)}, u32[]{:S(2)}, u32[]{:S(2)}) collective-permute-start(f32[8,64]{1,0:T(8,128)S(1)} %copy-done.6), channel_id=1, source_target_pairs={{0,30},{2,0},{4,2},{6,4},{8,6},{10,8},{12,10},{14,12},{16,14},{18,... | collective-permute-start | bytes 6152 | tf_op jit(solution)/shard_map/ppermute | solution.py:561
  12.8 2.8 %setup.1 = (bf16[8,64,192]{2,1,0:T(8,128)(2,1)S(1)}, bf16[4,128,384]{2,1,0:T(8,128)(2,1)S(1)}, f32[8,128]{1,0:T(8,128)S(1)}, f32[8,64]{1,0:T(8,128)S(1)}, f32[64...) custom-call(s32[8]{0:T(128)S(1)} %copy-done.5, f32[416,128]{1,0:T(8,128)S(1)} %get-tuple-element.60.refs_0_, ...), custom_call_target="tpu_custom_call" | custom-call | flops 330000000 | bytes 2992160 | tf_op jit(solution)/shard_map/setup/pallas_call | solution.py:547
  15.9 2.6 %collective-permute-done.refs_0_.before_ref = f32[8,64]{1,0:T(8,128)S(1)} collective-permute-done((f32[8,64]{1,0:T(8,128)S(1)}, f32[8,64]{1,0:T(8,128)S(1)}, u32[]{:S(2)}, u32[]{:S(2)}) %collective-permute-start) | collective-permute-done | bytes 2080 | tf_op jit(solution)/shard_map/ppermute | solution.py:561
  18.5 1.2 %first.1 = (f32[8,64,192]{2,1,0:T(8,128)S(1)}, f32[8,64,192]{2,1,0:T(8,128)S(1)}, f32[4,64,128]{2,1,0:T(8,128)S(1)}) custom-call(s32[8]{0:T(128)S(1)} %copy-done.5, f32[8,64]{1,0:T(8,128)S(1)} %collective-permute-done.refs_0_.before_ref, f32[8,64]{1,0:T(8,128)S(1)} %collective-permute-done.1.refs_1_.after_ref, f32[8,64,192]{2,1,0:T(8,128)S(1)} %get-tuple-element.62.refs_2_, ...), custom_call_target="tpu_custom_call" | custom-call | flops 330000000 | bytes 3084320 | tf_op jit(solution)/shard_map/first/pallas_call | solution.py:547
  19.7 1.5 %collective-permute-start.4 = (f32[4,64,128]{2,1,0:T(8,128)S(1)}, f32[4,64,128]{2,1,0:T(8,128)S(1)}, u32[]{:S(2)}, u32[]{:S(2)}) collective-permute-start(f32[4,64,128]{2,1,0:T(8,128)S(1)} %get-tuple-element.72.refs_0_), channel_id=1, source_target_pairs={{0,1},{1,0},{2,3},{3,2},{4,5},{5,4},{6,7},{7,6},{8,9},{9,8},{10,11... | collective-permute-start | bytes 393224 | tf_op jit(solution)/shard_map/ppermute | solution.py:561
  21.3 1.2 %smooth.1 = (f32[8,64,192]{2,1,0:T(8,128)S(1)}, f32[8,128]{1,0:T(8,128)S(1)}, f32[8,128]{1,0:T(8,128)S(1)}, f32[8,64,192]{2,1,0:T(8,128)S(1)}, f32[2,64,384]{2,1,0:T(8,128)S(1)}, /*index=5*/f32[2,64,384]{2,1,0:T(8,128)S(1)}) custom-call(s32[1]{0:T(128)} %bitcast.odd_ref, s32[8]{0:T(128)S(1)} %copy-done.5, f32[8,64,192]{2,1,0:T(8,128)S(1)} %bitcast.10, ...), custom_call_target="tpu_custom_call" | custom-call | flops 330000000 | bytes 2576420 | tf_op jit(solution)/shard_map/smooth/pallas_call | solution.py:547
  22.5 2.7 %collective-permute-start.6 = (f32[2,64,384]{2,1,0:T(8,128)S(1)}, f32[2,64,384]{2,1,0:T(8,128)S(1)}, u32[]{:S(2)}, u32[]{:S(2)}) collective-permute-start(f32[2,64,384]{2,1,0:T(8,128)S(1)} %get-tuple-element.75), channel_id=1, source_target_pairs={{2,4},{6,8},{10,12},{14,16},{18,20},{22,24},{26,28},{30,0},{4,2},{... | collective-permute-start | bytes 589832 | tf_op jit(solution)/shard_map/ppermute | solution.py:567
  25.2 3.4 %polar.3 = (f32[4,64,128]{2,1,0:T(8,128)S(1)}, f32[32,128]{1,0:T(8,128)S(1)}, f32[4,64,128]{2,1,0:T(8,128)S(1)}) custom-call(f32[8,64,192]{2,1,0:T(8,128)S(1)} %get-tuple-element.71.after_ref.inside_ref, f32[64,64]{1,0:T(8,128)S(1)} %copy-done.7, f32[4,64,128]{2,1,0:T(8,128)S(1)} %get-tuple-element.72.refs_0_, f32[4,64,128]{2,1,0:T(8,128)S(1)} %collective-permute-done.4.refs_1_), custom_call_target="tpu_custom_call" | custom-call | flops 3300000000 | bytes 950272 | tf_op jit(solution)/shard_map/polar/pallas_call | solution.py:547
  28.7 1.8 %collective-permute-start.7 = (f32[32,128]{1,0:T(8,128)S(1)}, f32[32,128]{1,0:T(8,128)S(1)}, u32[]{:S(2)}, u32[]{:S(2)}) collective-permute-start(f32[32,128]{1,0:T(8,128)S(1)} %get-tuple-element.73.after_ref.refs_1_), channel_id=1, source_target_pairs={{0,2},{2,0},{4,6},{6,4},{8,10},{10,8},{12,14},{14,12},{16,18},{18,... | collective-permute-start | bytes 49160 | tf_op jit(solution)/shard_map/ppermute | solution.py:604
  30.5 1.2 %ahead.2 = (f32[8,64,192]{2,1,0:T(8,128)S(1)}, f32[4,64,256]{2,1,0:T(8,128)S(1)}, f32[8,64,192]{2,1,0:T(8,128)S(1)}, f32[8,64,192]{2,1,0:T(8,128)S(1)}) custom-call(s32[1]{0:T(128)} %bitcast.odd_ref, f32[32,128]{1,0:T(8,128)S(1)} %get-tuple-element.73.after_ref.refs_1_, f32[8,64,192]{2,1,0:T(8,128)S(1)} %get-tuple-element.71.after_ref.inside_ref, ...), custom_call_target="tpu_custom_call" | custom-call | flops 330000000 | bytes 3624964 | tf_op jit(solution)/shard_map/ahead/pallas_call | solution.py:547
  32.5 1.1 %collective-permute-start.13 = (f32[4,64,256]{2,1,0:T(8,128)S(1)}, f32[4,64,256]{2,1,0:T(8,128)S(1)}, u32[]{:S(2)}, u32[]{:S(2)}) collective-permute-start(f32[4,64,256]{2,1,0:T(8,128)S(1)} %get-tuple-element.91.refs_0_), channel_id=1, source_target_pairs={{0,1},{1,0},{2,3},{3,2},{4,5},{5,4},{6,7},{7,6},{8,9},{9,8},{10,11... | collective-permute-start | bytes 786440 | tf_op jit(solution)/shard_map/ppermute | solution.py:561
  33.5 1.8 %collective-permute-start.12 = (f32[32,128]{1,0:T(8,128)S(1)}, f32[32,128]{1,0:T(8,128)S(1)}, u32[]{:S(2)}, u32[]{:S(2)}) collective-permute-start(f32[32,128]{1,0:T(8,128)S(1)} %add.3.refs_0_), channel_id=1, source_target_pairs={{0,24},{2,26},{4,28},{6,30},{8,16},{10,18},{12,20},{14,22},{16,8},... | collective-permute-start | bytes 49160 | tf_op jit(solution)/shard_map/ppermute | solution.py:604
  35.4 2.6 %collective-permute-start.10 = (f32[32,128]{1,0:T(8,128)S(1)}, f32[32,128]{1,0:T(8,128)S(1)}, u32[]{:S(2)}, u32[]{:S(2)}) collective-permute-start(f32[32,128]{1,0:T(8,128)S(1)} %add.3.refs_0_), channel_id=1, source_target_pairs={{0,8},{2,10},{4,12},{6,14},{8,0},{10,2},{12,4},{14,6},{16,24},{18,... | collective-permute-start | bytes 49160 | tf_op jit(solution)/shard_map/ppermute | solution.py:604
  37.9 1.1 %collective-permute-done.12.refs_3_ = f32[32,128]{1,0:T(8,128)S(1)} collective-permute-done((f32[32,128]{1,0:T(8,128)S(1)}, f32[32,128]{1,0:T(8,128)S(1)}, u32[]{:S(2)}, u32[]{:S(2)}) %collective-permute-start.12) | collective-permute-done | bytes 16416 | tf_op jit(solution)/shard_map/ppermute | solution.py:604
  41.4 2.4 %collective-permute-start.15 = (f32[2,64,384]{2,1,0:T(8,128)S(1)}, f32[2,64,384]{2,1,0:T(8,128)S(1)}, u32[]{:S(2)}, u32[]{:S(2)}) collective-permute-start(f32[2,64,384]{2,1,0:T(8,128)S(1)} %get-tuple-element.95), channel_id=1, source_target_pairs={{2,4},{6,8},{10,12},{14,16},{18,20},{22,24},{26,28},{30,0},{4,2},{... | collective-permute-start | bytes 589832 | tf_op jit(solution)/shard_map/ppermute | solution.py:567
  43.8 3.9 %polar.4 = (f32[4,64,128]{2,1,0:T(8,128)S(1)}, f32[32,128]{1,0:T(8,128)S(1)}, f32[4,64,128]{2,1,0:T(8,128)S(1)}) custom-call(f32[8,64,192]{2,1,0:T(8,128)S(1)} %get-tuple-element.88.after_ref.inside_ref, f32[64,64]{1,0:T(8,128)S(1)} %get-tuple-element.89.delta_ref, f32[4,64,128]{2,1,0:T(8,128)S(1)} %get-tuple-element.84.refs_0_.change_ref, ...), custom_call_target="tpu_custom_call" | custom-call | flops 330000000 | bytes 1474560 | tf_op jit(solution)/shard_map/polar/pallas_call | solution.py:547
  48.6 1.1 %collective-permute-start.16 = (f32[32,128]{1,0:T(8,128)S(1)}, f32[32,128]{1,0:T(8,128)S(1)}, u32[]{:S(2)}, u32[]{:S(2)}) collective-permute-start(f32[32,128]{1,0:T(8,128)S(1)} %get-tuple-element.93.after_ref.refs_1_), channel_id=1, source_target_pairs={{0,2},{2,0},{4,6},{6,4},{8,10},{10,8},{12,14},{14,12},{16,18},{18,... | collective-permute-start | bytes 49160 | tf_op jit(solution)/shard_map/ppermute | solution.py:604
  49.6 1.4 %ahead.3 = (f32[8,64,192]{2,1,0:T(8,128)S(1)}, f32[4,64,256]{2,1,0:T(8,128)S(1)}) custom-call(s32[1]{0:T(128)} %bitcast.odd_ref, f32[32,128]{1,0:T(8,128)S(1)} %get-tuple-element.93.after_ref.refs_1_, f32[8,64,192]{2,1,0:T(8,128)S(1)} %get-tuple-element.88.after_ref.inside_ref, f32[2,64,384]{2,1,0:T(8,128)S(1)} %collective-permute-done.14.near_ref, ...), custom_call_target="tpu_custom_call" | custom-call | flops 330000000 | bytes 2838532 | tf_op jit(solution)/shard_map/ahead/pallas_call | solution.py:547
  53.0 2.7 %collective-permute-start.21 = (f32[32,128]{1,0:T(8,128)S(1)}, f32[32,128]{1,0:T(8,128)S(1)}, u32[]{:S(2)}, u32[]{:S(2)}) collective-permute-start(f32[32,128]{1,0:T(8,128)S(1)} %add.4.refs_0_), channel_id=1, source_target_pairs={{0,24},{2,26},{4,28},{6,30},{8,16},{10,18},{12,20},{14,22},{16,8},... | collective-permute-start | bytes 49160 | tf_op jit(solution)/shard_map/ppermute | solution.py:604
  55.9 1.5 %collective-permute-start.19 = (f32[32,128]{1,0:T(8,128)S(1)}, f32[32,128]{1,0:T(8,128)S(1)}, u32[]{:S(2)}, u32[]{:S(2)}) collective-permute-start(f32[32,128]{1,0:T(8,128)S(1)} %add.4.refs_0_), channel_id=1, source_target_pairs={{0,8},{2,10},{4,12},{6,14},{8,0},{10,2},{12,4},{14,6},{16,24},{18,... | collective-permute-start | bytes 49160 | tf_op jit(solution)/shard_map/ppermute | solution.py:604
  57.3 1.1 %collective-permute-done.21.refs_3_ = f32[32,128]{1,0:T(8,128)S(1)} collective-permute-done((f32[32,128]{1,0:T(8,128)S(1)}, f32[32,128]{1,0:T(8,128)S(1)}, u32[]{:S(2)}, u32[]{:S(2)}) %collective-permute-start.21) | collective-permute-done | bytes 16416 | tf_op jit(solution)/shard_map/ppermute | solution.py:604
  58.5 1.8 %collective-permute-done.20.refs_2_ = f32[32,128]{1,0:T(8,128)S(1)} collective-permute-done((f32[32,128]{1,0:T(8,128)S(1)}, f32[32,128]{1,0:T(8,128)S(1)}, u32[]{:S(2)}, u32[]{:S(2)}) %collective-permute-start.20) | collective-permute-done | bytes 16416 | tf_op jit(solution)/shard_map/ppermute | solution.py:604
  60.8 3.9 %polar.5 = (f32[4,64,128]{2,1,0:T(8,128)S(1)}, f32[32,128]{1,0:T(8,128)S(1)}) custom-call(f32[8,64,192]{2,1,0:T(8,128)S(1)} %get-tuple-element.88.after_ref.inside_ref, f32[64,64]{1,0:T(8,128)S(1)} %get-tuple-element.99.delta_ref, f32[4,64,128]{2,1,0:T(8,128)S(1)} %get-tuple-element.100.change_ref, f32[4,64,128]{2,1,0:T(8,128)S(1)} %get-tuple-element.101.old_ref, ...), custom_call_target="tpu_custom_call" | custom-call | flops 330000000 | bytes 1343488 | tf_op jit(solution)/shard_map/polar/pallas_call | solution.py:547
  65.0 1.6 %collective-permute-start.23 = (f32[32,128]{1,0:T(8,128)S(1)}, f32[32,128]{1,0:T(8,128)S(1)}, u32[]{:S(2)}, u32[]{:S(2)}) collective-permute-start(f32[32,128]{1,0:T(8,128)S(1)} %get-tuple-element.108.refs_0_), channel_id=1, source_target_pairs={{0,2},{2,0},{4,6},{6,4},{8,10},{10,8},{12,14},{14,12},{16,18},{18,... | collective-permute-start | bytes 49160 | tf_op jit(solution)/shard_map/ppermute | solution.py:604
  66.6 1.3 %collective-permute-done.25.refs_3_ = f32[32,128]{1,0:T(8,128)S(1)} collective-permute-done((f32[32,128]{1,0:T(8,128)S(1)}, f32[32,128]{1,0:T(8,128)S(1)}, u32[]{:S(2)}, u32[]{:S(2)}) %collective-permute-start.25) | collective-permute-done | bytes 16416 | tf_op jit(solution)/shard_map/ppermute | solution.py:604
  68.6 1.5 %collective-permute-start.28 = (f32[32,128]{1,0:T(8,128)S(1)}, f32[32,128]{1,0:T(8,128)S(1)}, u32[]{:S(2)}, u32[]{:S(2)}) collective-permute-start(f32[32,128]{1,0:T(8,128)S(1)} %add.5.refs_0_), channel_id=1, source_target_pairs={{0,24},{2,26},{4,28},{6,30},{8,16},{10,18},{12,20},{14,22},{16,8},... | collective-permute-start | bytes 49160 | tf_op jit(solution)/shard_map/ppermute | solution.py:604
  70.9 2.1 %collective-permute-start.26 = (f32[32,128]{1,0:T(8,128)S(1)}, f32[32,128]{1,0:T(8,128)S(1)}, u32[]{:S(2)}, u32[]{:S(2)}) collective-permute-start(f32[32,128]{1,0:T(8,128)S(1)} %add.5.refs_0_), channel_id=1, source_target_pairs={{0,8},{2,10},{4,12},{6,14},{8,0},{10,2},{12,4},{14,6},{16,24},{18,... | collective-permute-start | bytes 49160 | tf_op jit(solution)/shard_map/ppermute | solution.py:604
  73.0 1.2 %rows.3 = (bf16[8,192,192]{2,1,0:T(8,128)(2,1)S(1)}, f32[8,64,192]{2,1,0:T(8,128)}) custom-call(f32[4,64,128]{2,1,0:T(8,128)S(1)} %get-tuple-element.103.mixed_ref, f32[4,64,128]{2,1,0:T(8,128)S(1)} %get-tuple-element.100.change_ref, f32[4,64,128]{2,1,0:T(8,128)S(1)} %get-tuple-element.104.forward_ref, f32[8,64,192]{2,1,0:T(8,128)S(1)} %get-tuple-element.97.tall_ref, ...), custom_call_target="tpu_custom_call" | custom-call | flops 330000000 | bytes 2162688 | tf_op jit(solution)/shard_map/rows/pallas_call | solution.py:547
  74.9 1.1 %last.1 = (f32[8,64,192]{2,1,0:T(8,128)}, f32[64,64]{1,0:T(8,128)}) custom-call(bf16[8,192,192]{2,1,0:T(8,128)(2,1)S(1)} %get-tuple-element.107.mixed_tall_ref, f32[32,128]{1,0:T(8,128)S(1)} %add.5.refs_0_, f32[32,128]{1,0:T(8,128)S(1)} %collective-permute-done.26.refs_1_, f32[32,128]{1,0:T(8,128)S(1)} %collective-permute-done.27.refs_2_, ...), custom_call_target="tpu_custom_call" | custom-call | flops 330000000 | bytes 1064960 | tf_op jit(solution)/shard_map/last/pallas_call | solution.py:547
  (61 shorter events, 10.3 us)
Async XLA Ops:
  1.5 11.3 %copy-start.2 = (f32[8,192,64]{1,2,0:T(8,128)S(1)}, f32[8,192,64]{1,2,0:T(8,128)}, u32[]{:S(2)}) copy-start(f32[8,192,64]{1,2,0:T(8,128)} %param.16) | copy-start | bytes 1179652
  1.5 11.3 %copy-start.3 = (f32[8,192,64]{1,2,0:T(8,128)S(1)}, f32[8,192,64]{1,2,0:T(8,128)}, u32[]{:S(2)}) copy-start(f32[8,192,64]{1,2,0:T(8,128)} %param.14) | copy-start | bytes 1179652
  1.5 11.3 %copy-start.5 = (s32[8]{0:T(128)S(1)}, s32[8]{0:T(128)}, u32[]{:S(2)}) copy-start(s32[8]{0:T(128)} %order_ref.5) | copy-start | bytes 100
  3.7 9.1 %collective-permute-start.2 = (f32[416,128]{1,0:T(8,128)S(1)}, f32[416,128]{1,0:T(8,128)S(1)}, u32[]{:S(2)}, u32[]{:S(2)}) collective-permute-start(f32[416,128]{1,0:T(8,128)S(1)} %get-tuple-element.61), channel_id=1, source_target_pairs={{0,1},{1,0},{2,3},{3,2},{4,5},{5,4},{6,7},{7,6},{8,9},{9,8},{10,11... | collective-permute-start | bytes 638984 | tf_op jit(solution)/shard_map/ppermute | solution.py:561
  8.7 9.8 %collective-permute-start.3 = (f32[384,128]{1,0:T(8,128)S(1)}, f32[384,128]{1,0:T(8,128)S(1)}, u32[]{:S(2)}, u32[]{:S(2)}) collective-permute-start(f32[384,128]{1,0:T(8,128)S(1)} %get-tuple-element.65), channel_id=1, source_target_pairs={{0,1},{1,0},{2,3},{3,2},{4,5},{5,4},{6,7},{7,6},{8,9},{9,8},{10,11... | collective-permute-start | bytes 589832 | tf_op jit(solution)/shard_map/ppermute | solution.py:561
  8.8 7.1 %collective-permute-start.1 = (f32[8,64]{1,0:T(8,128)S(1)}, f32[8,64]{1,0:T(8,128)S(1)}, u32[]{:S(2)}, u32[]{:S(2)}) collective-permute-start(f32[8,64]{1,0:T(8,128)S(1)} %copy-done.6), channel_id=1, source_target_pairs={{0,30},{2,0},{4,2},{6,4},{8,6},{10,8},{12,10},{14,12},{16,14},{18,... | collective-permute-start | bytes 6152 | tf_op jit(solution)/shard_map/ppermute | solution.py:561
  12.8 5.7 %collective-permute-start = (f32[8,64]{1,0:T(8,128)S(1)}, f32[8,64]{1,0:T(8,128)S(1)}, u32[]{:S(2)}, u32[]{:S(2)}) collective-permute-start(f32[8,64]{1,0:T(8,128)S(1)} %copy-done.6), channel_id=1, source_target_pairs={{0,2},{2,4},{4,6},{6,8},{8,10},{10,12},{12,14},{14,16},{16,18},{18... | collective-permute-start | bytes 6152 | tf_op jit(solution)/shard_map/ppermute | solution.py:561
  19.7 5.4 %collective-permute-start.4 = (f32[4,64,128]{2,1,0:T(8,128)S(1)}, f32[4,64,128]{2,1,0:T(8,128)S(1)}, u32[]{:S(2)}, u32[]{:S(2)}) collective-permute-start(f32[4,64,128]{2,1,0:T(8,128)S(1)} %get-tuple-element.72.refs_0_), channel_id=1, source_target_pairs={{0,1},{1,0},{2,3},{3,2},{4,5},{5,4},{6,7},{7,6},{8,9},{9,8},{10,11... | collective-permute-start | bytes 393224 | tf_op jit(solution)/shard_map/ppermute | solution.py:561
  22.4 8.1 %collective-permute-start.5 = (f32[2,64,384]{2,1,0:T(8,128)S(1)}, f32[2,64,384]{2,1,0:T(8,128)S(1)}, u32[]{:S(2)}, u32[]{:S(2)}) collective-permute-start(f32[2,64,384]{2,1,0:T(8,128)S(1)} %get-tuple-element.74), channel_id=1, source_target_pairs={{0,2},{4,6},{8,10},{12,14},{16,18},{20,22},{24,26},{28,30},{2,0},{... | collective-permute-start | bytes 589832 | tf_op jit(solution)/shard_map/ppermute | solution.py:567
  22.5 8.0 %collective-permute-start.6 = (f32[2,64,384]{2,1,0:T(8,128)S(1)}, f32[2,64,384]{2,1,0:T(8,128)S(1)}, u32[]{:S(2)}, u32[]{:S(2)}) collective-permute-start(f32[2,64,384]{2,1,0:T(8,128)S(1)} %get-tuple-element.75), channel_id=1, source_target_pairs={{2,4},{6,8},{10,12},{14,16},{18,20},{22,24},{26,28},{30,0},{4,2},{... | collective-permute-start | bytes 589832 | tf_op jit(solution)/shard_map/ppermute | solution.py:567
  28.6 3.2 %collective-permute-start.9 = (f32[32,128]{1,0:T(8,128)S(1)}, f32[32,128]{1,0:T(8,128)S(1)}, u32[]{:S(2)}, u32[]{:S(2)}) collective-permute-start(f32[32,128]{1,0:T(8,128)S(1)} %get-tuple-element.73.after_ref.refs_1_), channel_id=1, source_target_pairs={{0,6},{2,4},{4,2},{6,0},{8,14},{10,12},{12,10},{14,8},{16,22},{18,... | collective-permute-start | bytes 49160 | tf_op jit(solution)/shard_map/ppermute | solution.py:604
  28.7 3.8 %collective-permute-start.8 = (f32[32,128]{1,0:T(8,128)S(1)}, f32[32,128]{1,0:T(8,128)S(1)}, u32[]{:S(2)}, u32[]{:S(2)}) collective-permute-start(f32[32,128]{1,0:T(8,128)S(1)} %get-tuple-element.73.after_ref.refs_1_), channel_id=1, source_target_pairs={{0,4},{2,6},{4,0},{6,2},{8,12},{10,14},{12,8},{14,10},{16,20},{18,... | collective-permute-start | bytes 49160 | tf_op jit(solution)/shard_map/ppermute | solution.py:604
  28.7 3.7 %collective-permute-start.7 = (f32[32,128]{1,0:T(8,128)S(1)}, f32[32,128]{1,0:T(8,128)S(1)}, u32[]{:S(2)}, u32[]{:S(2)}) collective-permute-start(f32[32,128]{1,0:T(8,128)S(1)} %get-tuple-element.73.after_ref.refs_1_), channel_id=1, source_target_pairs={{0,2},{2,0},{4,6},{6,4},{8,10},{10,8},{12,14},{14,12},{16,18},{18,... | collective-permute-start | bytes 49160 | tf_op jit(solution)/shard_map/ppermute | solution.py:604
  32.5 11.3 %collective-permute-start.13 = (f32[4,64,256]{2,1,0:T(8,128)S(1)}, f32[4,64,256]{2,1,0:T(8,128)S(1)}, u32[]{:S(2)}, u32[]{:S(2)}) collective-permute-start(f32[4,64,256]{2,1,0:T(8,128)S(1)} %get-tuple-element.91.refs_0_), channel_id=1, source_target_pairs={{0,1},{1,0},{2,3},{3,2},{4,5},{5,4},{6,7},{7,6},{8,9},{9,8},{10,11... | collective-permute-start | bytes 786440 | tf_op jit(solution)/shard_map/ppermute | solution.py:561
  33.5 5.5 %collective-permute-start.12 = (f32[32,128]{1,0:T(8,128)S(1)}, f32[32,128]{1,0:T(8,128)S(1)}, u32[]{:S(2)}, u32[]{:S(2)}) collective-permute-start(f32[32,128]{1,0:T(8,128)S(1)} %add.3.refs_0_), channel_id=1, source_target_pairs={{0,24},{2,26},{4,28},{6,30},{8,16},{10,18},{12,20},{14,22},{16,8},... | collective-permute-start | bytes 49160 | tf_op jit(solution)/shard_map/ppermute | solution.py:604
  35.4 4.6 %collective-permute-start.11 = (f32[32,128]{1,0:T(8,128)S(1)}, f32[32,128]{1,0:T(8,128)S(1)}, u32[]{:S(2)}, u32[]{:S(2)}) collective-permute-start(f32[32,128]{1,0:T(8,128)S(1)} %add.3.refs_0_), channel_id=1, source_target_pairs={{0,16},{2,18},{4,20},{6,22},{8,24},{10,26},{12,28},{14,30},{16,0},... | collective-permute-start | bytes 49160 | tf_op jit(solution)/shard_map/ppermute | solution.py:604
  35.4 4.6 %collective-permute-start.10 = (f32[32,128]{1,0:T(8,128)S(1)}, f32[32,128]{1,0:T(8,128)S(1)}, u32[]{:S(2)}, u32[]{:S(2)}) collective-permute-start(f32[32,128]{1,0:T(8,128)S(1)} %add.3.refs_0_), channel_id=1, source_target_pairs={{0,8},{2,10},{4,12},{6,14},{8,0},{10,2},{12,4},{14,6},{16,24},{18,... | collective-permute-start | bytes 49160 | tf_op jit(solution)/shard_map/ppermute | solution.py:604
  41.3 8.4 %collective-permute-start.14 = (f32[2,64,384]{2,1,0:T(8,128)S(1)}, f32[2,64,384]{2,1,0:T(8,128)S(1)}, u32[]{:S(2)}, u32[]{:S(2)}) collective-permute-start(f32[2,64,384]{2,1,0:T(8,128)S(1)} %get-tuple-element.94), channel_id=1, source_target_pairs={{0,2},{4,6},{8,10},{12,14},{16,18},{20,22},{24,26},{28,30},{2,0},{... | collective-permute-start | bytes 589832 | tf_op jit(solution)/shard_map/ppermute | solution.py:567
  41.4 8.3 %collective-permute-start.15 = (f32[2,64,384]{2,1,0:T(8,128)S(1)}, f32[2,64,384]{2,1,0:T(8,128)S(1)}, u32[]{:S(2)}, u32[]{:S(2)}) collective-permute-start(f32[2,64,384]{2,1,0:T(8,128)S(1)} %get-tuple-element.95), channel_id=1, source_target_pairs={{2,4},{6,8},{10,12},{14,16},{18,20},{22,24},{26,28},{30,0},{4,2},{... | collective-permute-start | bytes 589832 | tf_op jit(solution)/shard_map/ppermute | solution.py:567
  47.7 3.3 %collective-permute-start.18 = (f32[32,128]{1,0:T(8,128)S(1)}, f32[32,128]{1,0:T(8,128)S(1)}, u32[]{:S(2)}, u32[]{:S(2)}) collective-permute-start(f32[32,128]{1,0:T(8,128)S(1)} %get-tuple-element.93.after_ref.refs_1_), channel_id=1, source_target_pairs={{0,6},{2,4},{4,2},{6,0},{8,14},{10,12},{12,10},{14,8},{16,22},{18,... | collective-permute-start | bytes 49160 | tf_op jit(solution)/shard_map/ppermute | solution.py:604
  48.2 3.7 %collective-permute-start.17 = (f32[32,128]{1,0:T(8,128)S(1)}, f32[32,128]{1,0:T(8,128)S(1)}, u32[]{:S(2)}, u32[]{:S(2)}) collective-permute-start(f32[32,128]{1,0:T(8,128)S(1)} %get-tuple-element.93.after_ref.refs_1_), channel_id=1, source_target_pairs={{0,4},{2,6},{4,0},{6,2},{8,12},{10,14},{12,8},{14,10},{16,20},{18,... | collective-permute-start | bytes 49160 | tf_op jit(solution)/shard_map/ppermute | solution.py:604
  48.6 3.4 %collective-permute-start.16 = (f32[32,128]{1,0:T(8,128)S(1)}, f32[32,128]{1,0:T(8,128)S(1)}, u32[]{:S(2)}, u32[]{:S(2)}) collective-permute-start(f32[32,128]{1,0:T(8,128)S(1)} %get-tuple-element.93.after_ref.refs_1_), channel_id=1, source_target_pairs={{0,2},{2,0},{4,6},{6,4},{8,10},{10,8},{12,14},{14,12},{16,18},{18,... | collective-permute-start | bytes 49160 | tf_op jit(solution)/shard_map/ppermute | solution.py:604
  52.0 8.8 %collective-permute-start.22 = (f32[4,64,256]{2,1,0:T(8,128)S(1)}, f32[4,64,256]{2,1,0:T(8,128)S(1)}, u32[]{:S(2)}, u32[]{:S(2)}) collective-permute-start(f32[4,64,256]{2,1,0:T(8,128)S(1)} %get-tuple-element.102.refs_0_), channel_id=1, source_target_pairs={{0,1},{1,0},{2,3},{3,2},{4,5},{5,4},{6,7},{7,6},{8,9},{9,8},{10,11... | collective-permute-start | bytes 786440 | tf_op jit(solution)/shard_map/ppermute | solution.py:561
  53.0 5.5 %collective-permute-start.21 = (f32[32,128]{1,0:T(8,128)S(1)}, f32[32,128]{1,0:T(8,128)S(1)}, u32[]{:S(2)}, u32[]{:S(2)}) collective-permute-start(f32[32,128]{1,0:T(8,128)S(1)} %add.4.refs_0_), channel_id=1, source_target_pairs={{0,24},{2,26},{4,28},{6,30},{8,16},{10,18},{12,20},{14,22},{16,8},... | collective-permute-start | bytes 49160 | tf_op jit(solution)/shard_map/ppermute | solution.py:604
  55.6 4.6 %collective-permute-start.20 = (f32[32,128]{1,0:T(8,128)S(1)}, f32[32,128]{1,0:T(8,128)S(1)}, u32[]{:S(2)}, u32[]{:S(2)}) collective-permute-start(f32[32,128]{1,0:T(8,128)S(1)} %add.4.refs_0_), channel_id=1, source_target_pairs={{0,16},{2,18},{4,20},{6,22},{8,24},{10,26},{12,28},{14,30},{16,0},... | collective-permute-start | bytes 49160 | tf_op jit(solution)/shard_map/ppermute | solution.py:604
  55.9 4.4 %collective-permute-start.19 = (f32[32,128]{1,0:T(8,128)S(1)}, f32[32,128]{1,0:T(8,128)S(1)}, u32[]{:S(2)}, u32[]{:S(2)}) collective-permute-start(f32[32,128]{1,0:T(8,128)S(1)} %add.4.refs_0_), channel_id=1, source_target_pairs={{0,8},{2,10},{4,12},{6,14},{8,0},{10,2},{12,4},{14,6},{16,24},{18,... | collective-permute-start | bytes 49160 | tf_op jit(solution)/shard_map/ppermute | solution.py:604
  64.7 3.2 %collective-permute-start.25 = (f32[32,128]{1,0:T(8,128)S(1)}, f32[32,128]{1,0:T(8,128)S(1)}, u32[]{:S(2)}, u32[]{:S(2)}) collective-permute-start(f32[32,128]{1,0:T(8,128)S(1)} %get-tuple-element.108.refs_0_), channel_id=1, source_target_pairs={{0,6},{2,4},{4,2},{6,0},{8,14},{10,12},{12,10},{14,8},{16,22},{18,... | collective-permute-start | bytes 49160 | tf_op jit(solution)/shard_map/ppermute | solution.py:604
  64.8 3.8 %collective-permute-start.24 = (f32[32,128]{1,0:T(8,128)S(1)}, f32[32,128]{1,0:T(8,128)S(1)}, u32[]{:S(2)}, u32[]{:S(2)}) collective-permute-start(f32[32,128]{1,0:T(8,128)S(1)} %get-tuple-element.108.refs_0_), channel_id=1, source_target_pairs={{0,4},{2,6},{4,0},{6,2},{8,12},{10,14},{12,8},{14,10},{16,20},{18,... | collective-permute-start | bytes 49160 | tf_op jit(solution)/shard_map/ppermute | solution.py:604
  65.0 3.6 %collective-permute-start.23 = (f32[32,128]{1,0:T(8,128)S(1)}, f32[32,128]{1,0:T(8,128)S(1)}, u32[]{:S(2)}, u32[]{:S(2)}) collective-permute-start(f32[32,128]{1,0:T(8,128)S(1)} %get-tuple-element.108.refs_0_), channel_id=1, source_target_pairs={{0,2},{2,0},{4,6},{6,4},{8,10},{10,8},{12,14},{14,12},{16,18},{18,... | collective-permute-start | bytes 49160 | tf_op jit(solution)/shard_map/ppermute | solution.py:604
  68.6 5.7 %collective-permute-start.28 = (f32[32,128]{1,0:T(8,128)S(1)}, f32[32,128]{1,0:T(8,128)S(1)}, u32[]{:S(2)}, u32[]{:S(2)}) collective-permute-start(f32[32,128]{1,0:T(8,128)S(1)} %add.5.refs_0_), channel_id=1, source_target_pairs={{0,24},{2,26},{4,28},{6,30},{8,16},{10,18},{12,20},{14,22},{16,8},... | collective-permute-start | bytes 49160 | tf_op jit(solution)/shard_map/ppermute | solution.py:604
  70.1 4.7 %collective-permute-start.27 = (f32[32,128]{1,0:T(8,128)S(1)}, f32[32,128]{1,0:T(8,128)S(1)}, u32[]{:S(2)}, u32[]{:S(2)}) collective-permute-start(f32[32,128]{1,0:T(8,128)S(1)} %add.5.refs_0_), channel_id=1, source_target_pairs={{0,16},{2,18},{4,20},{6,22},{8,24},{10,26},{12,28},{14,30},{16,0},... | collective-permute-start | bytes 49160 | tf_op jit(solution)/shard_map/ppermute | solution.py:604
  70.9 4.0 %collective-permute-start.26 = (f32[32,128]{1,0:T(8,128)S(1)}, f32[32,128]{1,0:T(8,128)S(1)}, u32[]{:S(2)}, u32[]{:S(2)}) collective-permute-start(f32[32,128]{1,0:T(8,128)S(1)} %add.5.refs_0_), channel_id=1, source_target_pairs={{0,8},{2,10},{4,12},{6,14},{8,0},{10,2},{12,4},{14,6},{16,24},{18,... | collective-permute-start | bytes 49160 | tf_op jit(solution)/shard_map/ppermute | solution.py:604
  (5 other events, 40.4 us)
